TPU v7x, 128 devices: a whole 4x4x4 slice. The times are simulated.
128 devices in a mesh: row: 16 (over x, z), col: 8 (over y, core).
Axes of the slice: x: 4, y: 4, z: 4, core: 2. Of those that a mesh axis runs over, the one named last changes fastest.
Arguments:
- grm: float32 [8, 2048, 16, 1024], P(None, 'row', None, 'col'), may hold values from -1 to 2, as said below
- dosages: bfloat16 [64, 8, 2048], P(None, None, 'row'), may hold values from -5 to 5
- slab_weight: float32 [1], replicated, may hold values from 0.05 to 0.2
- genetic_var: float32 [1], replicated, may hold values from 0.4 to 1.2
- noise_var: float32 [1], replicated, may hold values from 0.3 to 1
Outputs:
- factored: float32 [8, 2048, 16, 1024], P(None, 'row', None, 'col')
Inputs may be any that keep to these rules, and one draw needn't show every extreme that they name: `grm`: symmetric and positive definite.
All inputs are finite; a program needn't handle non-finite values.
Results may differ from a plain program's by a relative error of at most 0.0015.
Values may be sent and summed in bfloat16 or wider, within the bound.
A program may use at most 128 MiB of HBM per device.

v0:
```python
import jax
import jax.numpy as jnp
from jax import lax
from jax.sharding import PartitionSpec as P

KB = 4
MS = 64
PANELS = 2
PANEL = 512


def from_root(value, axis, source):
    kept = jnp.where(lax.axis_index(axis) == source, value, 0).astype(value.dtype)
    return lax.psum(kept, axis)


def per_device(grm, dosages, slab_weight, genetic_var, noise_var):
    prow = lax.axis_size("row")
    pcol = lax.axis_size("col")
    myrow = lax.axis_index("row")
    mycol = lax.axis_index("col")
    lbr, nb, lbc, _ = grm.shape
    rows = lbr * nb
    cols = lbc * nb
    grow = (
        jnp.arange(lbr, dtype=jnp.int32)[:, None] * (prow * nb)
        + myrow * nb
        + jnp.arange(nb, dtype=jnp.int32)[None, :]
    ).reshape(rows)
    gcol = (
        jnp.arange(lbc, dtype=jnp.int32)[:, None] * (pcol * nb)
        + mycol * nb
        + jnp.arange(nb, dtype=jnp.int32)[None, :]
    ).reshape(cols)
    everyone = lax.all_gather(dosages, "row", axis=2, tiled=True)
    row_dose = dosages.reshape(MS, rows)
    col_dose = lax.dynamic_slice_in_dim(
        everyone.reshape(MS, lbc, pcol * nb), mycol * nb, nb, 2
    ).reshape(MS, cols)
    product = lax.dot_general(
        row_dose, col_dose, (((0,), (0,)), ((), ())), preferred_element_type=jnp.float32
    )
    eye = (grow[:, None] == gcol[None, :]).astype(jnp.float32)
    work = (
        genetic_var[0] * (grm.reshape(rows, cols) + slab_weight[0] / MS * product)
        + noise_var[0] * eye
    )
    for p in range(PANELS):
        start_block = p * KB
        s1 = (start_block + KB) * nb
        local_col = start_block // pcol
        offset_col = start_block % pcol
        local_row = start_block // prow
        offset_row = start_block % prow
        column_block = work[:, local_col * nb : (local_col + 1) * nb]
        gathered = lax.all_gather(column_block, "col", axis=1, tiled=True)
        panel = gathered[:, offset_col * nb : offset_col * nb + PANEL]
        row_block = work[local_row * nb : (local_row + 1) * nb, :]
        panel_row = panel[local_row * nb : (local_row + 1) * nb, :]
        received = [
            (
                from_root(row_block, "row", offset_row + step),
                from_root(panel_row, "row", offset_row + step),
            )
            for step in range(KB)
        ]
        across = jnp.concatenate([item[0] for item in received], axis=0)
        diag_block = jnp.concatenate([item[1] for item in received], axis=0)
        factor = jnp.linalg.cholesky(diag_block)
        left = lax.linalg.triangular_solve(
            factor, panel, left_side=False, lower=True, transpose_a=True
        )
        right = lax.linalg.triangular_solve(factor, across, left_side=True, lower=True)
        left_tail = jnp.where(grow[:, None] >= s1, left, 0.0)
        right_tail = jnp.where(gcol[None, :] >= s1, right, 0.0)
        update = jnp.dot(
            left_tail,
            right_tail,
            precision=lax.Precision.HIGHEST,
            preferred_element_type=jnp.float32,
        )
        work = work - update
        owner = (mycol >= offset_col) & (mycol < offset_col + KB)
        within = jnp.clip(mycol - offset_col, 0, KB - 1)
        piece = lax.dynamic_slice_in_dim(left, within * nb, nb, 1)
        block_cols = gcol[local_col * nb : (local_col + 1) * nb]
        lowered = jnp.where(grow[:, None] >= block_cols[None, :], piece, 0.0)
        fresh = jnp.where(owner, lowered, work[:, local_col * nb : (local_col + 1) * nb])
        work = work.at[:, local_col * nb : (local_col + 1) * nb].set(fresh)
    return work.reshape(grm.shape)


def solution(mesh):
    in_specs = (P(None, "row", None, "col"), P(None, None, "row"), P(), P(), P())
    out_specs = P(None, "row", None, "col")
    return jax.shard_map(
        per_device, mesh=mesh, in_specs=in_specs, out_specs=out_specs, check_vma=False
    )
```

profile of v0, /device:TPU:6, one launch (start us, length us, event | category | flops | bytes accessed | tf_op | source)
XLA Modules:
  0.0 750.2 jit_solution(5383673248050360584)
XLA Ops:
  7.3 10.9 %copy.28 = f32[128,8,16,128]{3,1,2,0:T(8,128)} copy(f32[128,8,16,128]{3,2,1,0:T(8,128)} %bitcast.186) | data formatting | bytes 16777216
  18.2 9.3 %copy.14 = f32[1024,2048]{0,1:T(8,128)} copy(f32[1024,2048]{1,0:T(8,128)} %bitcast.177) | data formatting | bytes 16777216 | tf_op jit(solution)/shard_map/reshape | solution.py:45
  29.7 29.7 %all-gather.4.cloned.1.call-done = bf16[64,8,2048]{2,1,0:T(8,128)(2,1)} async-done(((bf16[64,8,128]{2,1,0:T(8,128)(2,1)}), bf16[64,8,2048]{2,1,0:T(8,128)(2,1)}) %all-gather.4.cloned.1.call-update) | async-done | bytes 2097168 | tf_op jit(solution)/shard_map/all_gather | solution.py:35
  59.3 2.7 reshape.203
  62.1 4.5 fusion.1
  66.6 3.4 copy-done
  71.0 3.3 slice_select_fusion.7
  74.2 28.5 %all-gather.6.cloned.1.call-done = f32[1024,1024]{0,1:T(8,128)} async-done(((f32[1024,128]{0,1:T(8,128)}), f32[1024,1024]{0,1:T(8,128)}) %all-gather.6.cloned.1.call-update) | async-done | bytes 4194320 | tf_op jit(solution)/shard_map/all_gather | solution.py:56
  102.7 1.9 slice_select_fusion.12
  105.9 115.5 %all-reduce.8.cloned.1.call-done = (f32[128,2048]{0,1:T(8,128)}, f32[128,2048]{0,1:T(8,128)}, f32[128,2048]{0,1:T(8,128)}, f32[128,2048]{0,1:T(8,128)}, f32[128,...) async-done(((f32[128,2048]{0,1:T(8,128)}, f32[128,2048]{0,1:T(8,128)}, f32[128,2048]{0,1:T(8,128)}, f32[128,2048]{0,1:T(8,128)}, ...) | async-done | bytes 5242896 | tf_op jit(solution)/shard_map/psum | solution.py:14
  223.4 1.0 constant_dynamic-update-slice_fusion.1
  225.9 11.7 %cholesky.286 = f32[128,128]{1,0:T(8,128)S(1)} custom-call(f32[128,128]{1,0:T(8,128)S(1)} %cholesky.426), custom_call_target="Cholesky" | custom-call | tf_op jit(solution)/shard_map/jit(cholesky)/cholesky | solution.py:69
  237.8 9.8 %custom-call.31 = f32[1,128,128]{1,2,0:T(8,128)S(1)} custom-call(f32[1,128,128]{2,1,0:T(8,128)S(1)} %get-tuple-element.137), custom_call_target="InvertDiagBlocksLowerTriangular" | custom-call | tf_op jit(solution)/shard_map/jit(cholesky)/cholesky | solution.py:69
  248.3 11.7 %cholesky.305 = f32[128,128]{1,0:T(8,128)S(1)} custom-call(f32[128,128]{1,0:T(8,128)S(1)} %cholesky.430), custom_call_target="Cholesky" | custom-call | tf_op jit(solution)/shard_map/jit(cholesky)/cholesky | solution.py:69
  260.1 10.2 %custom-call.32 = f32[1,128,128]{1,2,0:T(8,128)S(1)} custom-call(f32[1,128,128]{2,1,0:T(8,128)S(1)} %get-tuple-element.134), custom_call_target="InvertDiagBlocksLowerTriangular" | custom-call | tf_op jit(solution)/shard_map/jit(cholesky)/cholesky | solution.py:69
  271.0 11.7 %cholesky.326 = f32[128,128]{1,0:T(8,128)S(1)} custom-call(f32[128,128]{1,0:T(8,128)S(1)} %cholesky.435), custom_call_target="Cholesky" | custom-call | tf_op jit(solution)/shard_map/jit(cholesky)/cholesky | solution.py:69
  282.7 9.8 %custom-call.33 = f32[1,128,128]{1,2,0:T(8,128)S(1)} custom-call(f32[1,128,128]{2,1,0:T(8,128)S(1)} %get-tuple-element.131), custom_call_target="InvertDiagBlocksLowerTriangular" | custom-call | tf_op jit(solution)/shard_map/jit(cholesky)/cholesky | solution.py:69
  293.1 11.7 %cholesky.343 = f32[128,128]{1,0:T(8,128)S(1)} custom-call(f32[128,128]{1,0:T(8,128)S(1)} %convolution_subtract_fusion.13), custom_call_target="Cholesky" | custom-call | tf_op jit(solution)/shard_map/jit(cholesky)/cholesky | solution.py:69
  309.5 7.6 %while.10 = (s32[]{:T(128)}, f32[512,512]{1,0:T(8,128)S(1)}, s32[4,2]{0,1:T(2,128)S(1)}, f32[4,128,128]{2,1,0:T(8,128)S(1)}, s32[]{:T(128)}) while((s32[]{:T(128)}, f32[512,512]{1,0:T(8,128)S(1)}, s32[4,2]{0,1:T(2,128)S(1)}, f32[4,128,128]{2,1,0:T(8,128)S(1)}, s32[]{:T(128)}) %tuple.83), condition=%wide.while_cond.2, body=%wide.while_body.2.sunk | while | flops 2 | bytes 131189 | solution.py:70
  310.1 1.3 bitcast_dynamic-update-slice_fusion.4
  312.0 1.3 bitcast_dynamic-update-slice_fusion.4
  314.0 1.3 bitcast_dynamic-update-slice_fusion.4
  315.9 1.3 bitcast_dynamic-update-slice_fusion.4
  317.2 39.3 %custom-call.34 = f32[4,128,128]{1,2,0:T(8,128)S(1)} custom-call(f32[4,128,128]{2,1,0:T(8,128)S(1)} %get-tuple-element.60), custom_call_target="InvertDiagBlocksLowerTriangular" | custom-call | tf_op jit(solution)/shard_map/triangular_solve/custom-call.3 | solution.py:70
  356.5 2.3 fusion.117
  358.8 3.1 convolution_subtract_fusion.3
  361.9 1.1 fusion.118
  363.0 3.6 convolution_subtract_fusion.1
  366.6 1.1 fusion.120
  367.7 5.7 fusion.33
  373.4 1.1 fusion.122
  377.7 1.2 fusion.63
  379.9 16.2 %fusion.17 = f32[1024,2048]{0,1:T(8,128)} fusion(f32[1024,2048]{0,1:T(8,128)S(1)} %bitcast.174, f32[128,2048]{1,0:T(8,128)S(1)} %fusion.122, f32[128,2048]{1,0:T(8,128)S(1)} %fusion.120, f32[128,2048]{1,0:T(8,128)S(1)} %fusion.118, f32[128,2048]{1,0:T(8,128)S(1)} %fusion.117, pred[2048]{0:T(1024)(128)(4,1)S(1)} %get-tuple-element.141, ...), kind=kOutput, calls=%fused_computation.25 | convolution fusion | flops 12893290496 | bytes 23071744 | tf_op jit(solution)/shard_map/dot_general | solution.py:76
  396.1 2.9 constant_dynamic-update-slice_fusion.12
  399.2 3.3 slice_select_fusion.3
  402.5 28.5 %all-gather.8.cloned.1.call-done = f32[1024,1024]{0,1:T(8,128)} async-done(((f32[1024,128]{0,1:T(8,128)}), f32[1024,1024]{0,1:T(8,128)}) %all-gather.8.cloned.1.call-update) | async-done | bytes 4194320 | tf_op jit(solution)/shard_map/all_gather | solution.py:56
  431.0 1.9 slice_select_fusion.8
  433.0 117.2 %all-reduce.6.cloned.1.call-done = (f32[128,2048]{0,1:T(8,128)}, f32[128,2048]{0,1:T(8,128)}, f32[128,2048]{0,1:T(8,128)}, f32[128,2048]{0,1:T(8,128)}, f32[128,...) async-done(((f32[128,2048]{0,1:T(8,128)}, f32[128,2048]{0,1:T(8,128)}, f32[128,2048]{0,1:T(8,128)}, f32[128,2048]{0,1:T(8,128)}, ...) | async-done | bytes 5242896 | tf_op jit(solution)/shard_map/psum | solution.py:14
  551.1 1.0 constant_dynamic-update-slice_fusion.6
  553.1 1.0 constant_dynamic-update-slice_fusion.4
  554.7 11.7 %cholesky.358 = f32[128,128]{1,0:T(8,128)S(1)} custom-call(f32[128,128]{1,0:T(8,128)S(1)} %cholesky.439), custom_call_target="Cholesky" | custom-call | tf_op jit(solution)/shard_map/jit(cholesky)/cholesky | solution.py:69
  566.5 9.8 %custom-call.36 = f32[1,128,128]{1,2,0:T(8,128)S(1)} custom-call(f32[1,128,128]{2,1,0:T(8,128)S(1)} %get-tuple-element.127), custom_call_target="InvertDiagBlocksLowerTriangular" | custom-call | tf_op jit(solution)/shard_map/jit(cholesky)/cholesky | solution.py:69
  577.0 11.7 %cholesky.377 = f32[128,128]{1,0:T(8,128)S(1)} custom-call(f32[128,128]{1,0:T(8,128)S(1)} %cholesky.443), custom_call_target="Cholesky" | custom-call | tf_op jit(solution)/shard_map/jit(cholesky)/cholesky | solution.py:69
  588.8 10.2 %custom-call.37 = f32[1,128,128]{1,2,0:T(8,128)S(1)} custom-call(f32[1,128,128]{2,1,0:T(8,128)S(1)} %get-tuple-element.124), custom_call_target="InvertDiagBlocksLowerTriangular" | custom-call | tf_op jit(solution)/shard_map/jit(cholesky)/cholesky | solution.py:69
  599.6 11.7 %cholesky.398 = f32[128,128]{1,0:T(8,128)S(1)} custom-call(f32[128,128]{1,0:T(8,128)S(1)} %cholesky.448), custom_call_target="Cholesky" | custom-call | tf_op jit(solution)/shard_map/jit(cholesky)/cholesky | solution.py:69
  611.4 9.8 %custom-call.38 = f32[1,128,128]{1,2,0:T(8,128)S(1)} custom-call(f32[1,128,128]{2,1,0:T(8,128)S(1)} %get-tuple-element.121), custom_call_target="InvertDiagBlocksLowerTriangular" | custom-call | tf_op jit(solution)/shard_map/jit(cholesky)/cholesky | solution.py:69
  621.8 11.9 %cholesky.415 = f32[128,128]{1,0:T(8,128)S(1)} custom-call(f32[128,128]{1,0:T(8,128)S(1)} %convolution_subtract_fusion.12), custom_call_target="Cholesky" | custom-call | tf_op jit(solution)/shard_map/jit(cholesky)/cholesky | solution.py:69
  638.8 7.6 %while.11 = (s32[]{:T(128)}, f32[512,512]{1,0:T(8,128)S(1)}, s32[4,2]{0,1:T(2,128)S(1)}, f32[4,128,128]{2,1,0:T(8,128)S(1)}, s32[]{:T(128)}) while((s32[]{:T(128)}, f32[512,512]{1,0:T(8,128)S(1)}, s32[4,2]{0,1:T(2,128)S(1)}, f32[4,128,128]{2,1,0:T(8,128)S(1)}, s32[]{:T(128)}) %tuple.101), condition=%wide.while_cond.2.clone, body=%wide.while_body.2.clone.sunk | while | flops 2 | bytes 131189 | solution.py:70
  639.4 1.3 bitcast_dynamic-update-slice_fusion.5
  641.3 1.3 bitcast_dynamic-update-slice_fusion.5
  643.2 1.3 bitcast_dynamic-update-slice_fusion.5
  645.1 1.3 bitcast_dynamic-update-slice_fusion.5
  646.4 39.3 %custom-call.39 = f32[4,128,128]{1,2,0:T(8,128)S(1)} custom-call(f32[4,128,128]{2,1,0:T(8,128)S(1)} %get-tuple-element.62), custom_call_target="InvertDiagBlocksLowerTriangular" | custom-call | tf_op jit(solution)/shard_map/triangular_solve/custom-call.3 | solution.py:70
  685.7 2.3 fusion.124
  688.0 3.1 convolution_subtract_fusion.2
  691.2 1.1 fusion.125
  692.3 3.6 convolution_subtract_fusion
  695.8 1.1 fusion.127
  696.9 5.5 fusion.30
  702.5 1.1 fusion.129
  706.8 1.2 fusion.60
  708.8 17.5 %fusion.16 = f32[1024,2048]{0,1:T(8,128)S(1)} fusion(f32[1024,2048]{0,1:T(8,128)} %get-tuple-element.96, f32[128,2048]{1,0:T(8,128)S(1)} %fusion.129, f32[128,2048]{1,0:T(8,128)S(1)} %fusion.127, f32[128,2048]{1,0:T(8,128)S(1)} %fusion.125, f32[128,2048]{1,0:T(8,128)S(1)} %fusion.124, pred[2048]{0:T(1024)(128)(4,1)S(1)} %get-tuple-element.140, ...), kind=kOutput, calls=%fused_computation.24 | convolution fusion | flops 12893290496 | bytes 23071744 | tf_op jit(solution)/shard_map/dot_general | solution.py:76
  727.2 5.3 copy.18
  732.5 10.7 %copy.11 = f32[8,128,16,128]{3,2,1,0:T(8,128)} copy(f32[8,128,16,128]{1,0,3,2:T(8,128)} %bitcast.176) | data formatting | bytes 16777216 | tf_op jit(solution)/shard_map/reshape | solution.py:90
  (121 shorter events, 32.4 us)
Async XLA Ops:
  6.5 52.8 %all-gather.4.cloned.1.call-start = ((), (), s32[]{:S(2)}) async-start(), calls=%async_computation | async-start | bytes 2228224 | tf_op jit(solution)/shard_map/all_gather | solution.py:35
  7.3 95.5 %all-gather.6.cloned.1.call-start = ((), (), s32[]{:S(2)}) async-start(), calls=%async_computation.1 | async-start | bytes 4718592 | tf_op jit(solution)/shard_map/all_gather | solution.py:56
  27.5 34.6 %copy-start.7 = (bf16[64,8,128]{2,1,0:T(8,128)(2,1)S(1)}, bf16[64,8,128]{2,1,0:T(8,128)(2,1)}, u32[]{:S(2)}) copy-start(bf16[64,8,128]{2,1,0:T(8,128)(2,1)} %param.15) | copy-start | bytes 393220
  66.6 3.4 copy-start
  70.9 150.5 %all-reduce.8.cloned.1.call-start = ((), (), s32[]{:S(2)}) async-start(), calls=%async_computation.4 | async-start | bytes 10485760 | tf_op jit(solution)/shard_map/psum | solution.py:14
  104.7 326.3 %all-gather.8.cloned.1.call-start = ((), (), s32[]{:S(2)}) async-start(), calls=%async_computation.2 | async-start | bytes 4718592 | tf_op jit(solution)/shard_map/all_gather | solution.py:56
  358.8 4.2 copy-start.4
  363.0 4.7 copy-start.3
  367.7 6.8 copy-start.1
  374.5 5.3 slice-start
  377.7 2.2 slice-start.1
  399.0 151.1 %all-reduce.6.cloned.1.call-start = ((), (), s32[]{:S(2)}) async-start(), calls=%async_computation.3 | async-start | bytes 10485760 | tf_op jit(solution)/shard_map/psum | solution.py:14
  688.0 4.2 copy-start.6
  692.3 4.7 copy-start.5
  696.9 6.6 copy-start.2
Sparse Core Ops, SparseCore 0:
  9.5 49.7 all-gather.3
  71.0 31.6 all-gather.5
  107.1 114.3 all-reduce.7
  399.1 31.8 all-gather.7
  435.7 114.3 all-reduce.5
where the time goes:
time: 758 us; the launch traced here: 750 us
  waiting for transfers between devices  320 us (42%)
  other arithmetic  254 us (34%)
  matrix products  87.5 us (12%)
  local copies, waits for them, and re-layouts  67.3 us (9%)
  between operations  21.2 us (3%)
    psum x2, waiting for transfers between devices, from_root(): return lax.psum(kept, axis)  233 us
    another operation x29, other arithmetic, per_device(): factor = jnp.linalg.cholesky(diag_block)  158 us
    another operation x7, other arithmetic, per_device(): lax.linalg.triangular_solve(factor, panel, left_side=False, lower=True, t...  79.4 us
    all_gather x2, waiting for transfers between devices, per_device(): gathered = lax.all_gather(column_block, 'col', axis=1, tiled=True)  57 us
    another operation x14, matrix products, per_device(): lax.linalg.triangular_solve(factor, across, left_side=True, lower=True)  35.6 us
    dot_general x2, matrix products, per_device(): jnp.dot(left_tail, right_tail, precision=lax.Precision.HIGHEST, preferred...  33.7 us
    all_gather x1, waiting for transfers between devices, per_device(): everyone = lax.all_gather(dosages, 'row', axis=2, tiled=True)  29.7 us
    unnamed x28, local copies, waits for them, and re-layouts  25.6 us
  transfers between devices with their start and end apart: 5, of which 5 were waited for; matrix products, arithmetic and copies ran while one was open for 4% of the time, Pallas kernels for 0%

commit v1 on v0

v1 whole, which is shorter than its diff:
```python
import functools

import jax
import jax.numpy as jnp
from jax import lax
from jax.experimental import pallas as pl
from jax.experimental.pallas import tpu as pltpu
from jax.sharding import PartitionSpec as P

NB = 128
MS = 64
PANEL = 512
BOTH = 1024
HI = lax.Precision.HIGHEST
F32 = jnp.float32
BF16 = jnp.bfloat16


def lane_bcast(x, j):
    return jnp.broadcast_to(x[:, j : j + 1], (8, 128))


def sub_bcast(x, i):
    return jnp.broadcast_to(x[i : i + 1, :], (8, 128))


def inverse_factor_128(slabs):
    lane = lax.broadcasted_iota(jnp.int32, (8, 128), 1)
    sub = lax.broadcasted_iota(jnp.int32, (8, 128), 0)
    slabs = list(slabs)
    for s in range(16):
        cols = {t: [lane_bcast(slabs[t], 8 * s + k) for k in range(8)] for t in range(s, 16)}
        b = {(i, k): sub_bcast(cols[s][k], i) for k in range(8) for i in range(k, 8)}
        here = (lane >= 8 * s) & (lane < 8 * s + 8)
        ident = (lane - 8 * s == sub).astype(F32)
        rp = jnp.where(here, ident, slabs[s])
        r = [sub_bcast(rp, i) for i in range(8)]
        inv = [None] * 8
        l = {}
        for j in range(8):
            inv[j] = 1.0 / b[j, j]
            for i in range(j + 1, 8):
                l[i, j] = b[i, j] * inv[j]
            for i in range(j + 1, 8):
                for m in range(j + 1, i + 1):
                    b[i, m] = b[i, m] - l[i, j] * b[m, j]
                r[i] = r[i] - l[i, j] * r[j]
        out = None
        for i in range(8):
            v = r[i] * lax.rsqrt(b[i, i])
            out = v if out is None else jnp.where(sub == i, v, out)
        w = [r[i] * inv[i] for i in range(8)]
        for j in range(7, 0, -1):
            for i in range(j):
                w[i] = w[i] - l[j, i] * w[j]
        slabs[s] = jnp.where(lane < 8 * s + 8, out, 0.0)
        for t in range(s + 1, 16):
            acc = cols[t][0] * w[0]
            for k in range(1, 8):
                acc = acc + cols[t][k] * w[k]
            slabs[t] = jnp.where(here, 0.0, slabs[t]) - acc
    return slabs


def factor_kernel(scal_ref, p_ref, zp_ref, v_ref):
    gv, sw, nv = scal_ref[0], scal_ref[1], scal_ref[2]
    n = BOTH
    nb = n // NB
    zp = zp_ref[...]
    for i in range(nb):
        s = lax.dot_general(zp[:, i * NB : (i + 1) * NB], zp, (((0,), (0,)), ((), ())), preferred_element_type=F32)
        row = lax.broadcasted_iota(jnp.int32, (NB, n), 0) + i * NB
        col = lax.broadcasted_iota(jnp.int32, (NB, n), 1)
        g = jnp.concatenate([p_ref[i, k] for k in range(nb)], axis=1)
        v_ref[i * NB : (i + 1) * NB, :] = gv * (g + sw / MS * s) + jnp.where(row == col, nv, 0.0)
    for k in range(nb):
        kb = k * NB
        slabs = [v_ref[kb + 8 * s : kb + 8 * s + 8, kb : kb + NB] for s in range(16)]
        vk = jnp.concatenate(inverse_factor_128(slabs), axis=0)
        parts = []
        if k > 0:
            parts.append(jnp.dot(vk, v_ref[kb : kb + NB, :kb], precision=HI, preferred_element_type=F32))
        parts.append(vk)
        if k < nb - 1:
            right = jnp.dot(vk, v_ref[kb : kb + NB, kb + NB :], precision=HI, preferred_element_type=F32)
            parts.append(right)
            u = jnp.concatenate(parts, axis=1)
            upd = lax.dot_general(right, u, (((0,), (0,)), ((), ())), precision=HI, preferred_element_type=F32)
            if k > 0:
                v_ref[kb + NB :, :kb] = v_ref[kb + NB :, :kb] - upd[:, :kb]
                v_ref[kb : kb + NB, :kb] = parts[0]
            v_ref[kb + NB :, kb : kb + NB] = -upd[:, kb : kb + NB]
            v_ref[kb + NB :, kb + NB :] = v_ref[kb + NB :, kb + NB :] - upd[:, kb + NB :]
            v_ref[kb : kb + NB, kb : kb + NB] = vk
            v_ref[kb : kb + NB, kb + NB :] = jnp.zeros((NB, n - kb - NB), F32)
        else:
            v_ref[kb : kb + NB, :] = jnp.concatenate(parts, axis=1)


def factor(scal, p_raw, zp):
    return pl.pallas_call(
        factor_kernel,
        out_shape=jax.ShapeDtypeStruct((BOTH, BOTH), F32),
        in_specs=[
            pl.BlockSpec(memory_space=pltpu.SMEM),
            pl.BlockSpec(memory_space=pltpu.VMEM),
            pl.BlockSpec(memory_space=pltpu.VMEM),
        ],
        out_specs=pl.BlockSpec(memory_space=pltpu.VMEM),
        compiler_params=pltpu.CompilerParams(vmem_limit_bytes=48 * 1024 * 1024),
        cost_estimate=pl.CostEstimate(flops=20_000_000_000, bytes_accessed=8_000_000, transcendentals=0),
        name="panel_factor",
    )(scal, p_raw, zp)


def split(x):
    hi = x.astype(BF16)
    return hi, (x - hi.astype(F32)).astype(BF16)


NN = (((1,), (0,)), ((), ()))
NT = (((1,), (1,)), ((), ()))
TN = (((0,), (0,)), ((), ()))


def dot3(ah, al, bh, bl, dims):
    d = functools.partial(lax.dot_general, dimension_numbers=dims, preferred_element_type=F32)
    return d(ah, bh) + (d(ah, bl) + d(al, bh))


def update_kernel(
    scal_ref, zr_ref, zp_ref, zc_ref, g_hbm, left_hbm, right_hbm, v_hbm, out_hbm,
    gbuf, abuf, rbuf, vbuf, vh, vl, ah, al, wh, wl, sems,
):
    gv, sw, nv = scal_ref[0], scal_ref[1], scal_ref[2]
    swn = sw / MS
    row = lax.axis_index("row")
    col = lax.axis_index("col")
    copies_v = pltpu.make_async_copy(v_hbm, vbuf, sems.at[0])
    copies_v.start()
    copies_l = [
        pltpu.make_async_copy(left_hbm.at[k], abuf.at[:, k * NB : (k + 1) * NB], sems.at[1 + k]) for k in range(8)
    ]
    for c in copies_l:
        c.start()
    copies_r = [
        pltpu.make_async_copy(
            right_hbm.at[8 * h + k], rbuf.at[:, h, :, k * NB : (k + 1) * NB], sems.at[9 + 8 * h + k]
        )
        for h in range(2)
        for k in range(8)
    ]
    copy_g = pltpu.make_async_copy(g_hbm, gbuf, sems.at[25])
    for c in copies_r:
        c.start()
    copy_g.start()

    zr = zr_ref[...]
    zp = zp_ref[...]
    copies_v.wait()
    for J in range(4):
        h, lo = split(vbuf[J * 256 : (J + 1) * 256, :])
        vh[J * 256 : (J + 1) * 256, :] = h
        vl[J * 256 : (J + 1) * 256, :] = lo
    for c in copies_l:
        c.wait()

    @pl.loop(0, 8)
    def _(rb):
        at = pl.ds(pl.multiple_of(rb * NB, NB), NB)
        s = lax.dot_general(zr_ref[:, at], zp, TN, preferred_element_type=F32)
        me = row + 16 * rb
        r_at = lax.broadcasted_iota(jnp.int32, (NB, BOTH), 0) + me * NB
        c_at = lax.broadcasted_iota(jnp.int32, (NB, BOTH), 1)
        a = gv * (abuf[at, :] + swn * s) + jnp.where(r_at == c_at, nv, 0.0)
        h, lo = split(a)
        ah[at, :] = h
        al[at, :] = lo

    for J in range(4):
        K = (J + 1) * 256
        js = slice(J * 256, (J + 1) * 256)
        abuf[:, js] = dot3(ah[:, :K], al[:, :K], vh[js, :K], vl[js, :K], NT)

    keep1 = jnp.where(row >= 4, 1.0, 0.0)
    keep2 = jnp.where(row >= 8, 1.0, 0.0)
    for rb in range(8):
        at = slice(rb * NB, (rb + 1) * NB)
        x = abuf[at, :]
        if rb == 0:
            c_at = lax.broadcasted_iota(jnp.int32, (NB, BOTH), 1)
            x = x * jnp.where(c_at < PANEL, keep1, keep2)
        h, lo = split(x)
        ah[at, :] = h
        al[at, :] = lo

    for J in range(4):
        js = slice(J * 256, (J + 1) * 256)
        K = slice(J * 256, BOTH)
        w = dot3(ah[:, K], al[:, K], vh[K, js], vl[K, js], NN)
        h, lo = split(w)
        wh[:, js] = h
        wl[:, js] = lo

    for c in copies_r:
        c.wait()
    copy_g.wait()
    g2 = gbuf.reshape(16384, NB)

    @pl.loop(0, 8)
    def _(p):
        zc = zc_ref[:, pl.ds(pl.multiple_of(p * 256, 256), 256)]
        s = lax.dot_general(zc, zp, TN, preferred_element_type=F32)
        raw = jnp.concatenate([rbuf[p, 0], rbuf[p, 1]], axis=0)
        rh, rl = split(gv * (raw + swn * s))
        upd = dot3(wh[...], wl[...], rh, rl, NT)
        own = lax.dot_general(zr, zc, TN, preferred_element_type=F32)
        eye = jnp.where(
            lax.broadcasted_iota(jnp.int32, (NB, NB), 0) == lax.broadcasted_iota(jnp.int32, (NB, NB), 1), nv, 0.0
        )
        for rb in range(8):
            rs = slice(rb * NB, (rb + 1) * NB)
            for e in range(2):
                es = slice(e * NB, (e + 1) * NB)
                lc = 2 * p + e
                at = pl.ds(rb * 2048 + lc, NB, stride=16)
                on = jnp.where(16 * rb + row == 8 * lc + col, 1.0, 0.0)
                g2[at, :] = gv * (g2[at, :] + swn * own[rs, es]) - upd[rs, es] + on * eye

    r_at = lax.broadcasted_iota(jnp.int32, (NB, NB), 0) + row * NB
    c_at = lax.broadcasted_iota(jnp.int32, (NB, NB), 1) + col * NB
    mine = pl.ds(pl.multiple_of(col * NB, NB), NB)
    for rb in range(8):
        x = abuf[rb * NB : (rb + 1) * NB, mine]
        if rb == 0:
            x = jnp.where(r_at >= c_at, x, 0.0)
        g2[pl.ds(rb * 2048, NB, stride=16), :] = x
    done = pltpu.make_async_copy(gbuf, out_hbm, sems.at[26])
    done.start()
    done.wait()


def update(scal, zr, zp, zc, g, left, right, v):
    anyspec = pl.BlockSpec(memory_space=pl.ANY)
    vmem = pl.BlockSpec(memory_space=pltpu.VMEM)
    return pl.pallas_call(
        update_kernel,
        out_shape=jax.ShapeDtypeStruct((1024, 16, NB), F32),
        in_specs=[pl.BlockSpec(memory_space=pltpu.SMEM), vmem, vmem, vmem, anyspec, anyspec, anyspec, anyspec],
        out_specs=anyspec,
        scratch_shapes=[
            pltpu.VMEM((1024, 16, NB), F32),
            pltpu.VMEM((1024, BOTH), F32),
            pltpu.VMEM((8, 2, NB, BOTH), F32),
            pltpu.VMEM((BOTH, BOTH), F32),
            pltpu.VMEM((BOTH, BOTH), BF16),
            pltpu.VMEM((BOTH, BOTH), BF16),
            pltpu.VMEM((1024, BOTH), BF16),
            pltpu.VMEM((1024, BOTH), BF16),
            pltpu.VMEM((1024, BOTH), BF16),
            pltpu.VMEM((1024, BOTH), BF16),
            pltpu.SemaphoreType.DMA((27,)),
        ],
        compiler_params=pltpu.CompilerParams(vmem_limit_bytes=60 * 1024 * 1024),
        cost_estimate=pl.CostEstimate(flops=25_000_000_000, bytes_accessed=36_000_000, transcendentals=0),
        name="trailing_update",
    )(scal, zr, zp, zc, g, left, right, v)


TRANSPOSE = [((8 * h + c) * 8 + k, (8 * h + k) * 8 + c) for h in range(2) for c in range(8) for k in range(8)]


def per_device(grm, dosages, slab_weight, genetic_var, noise_var):
    mycol = lax.axis_index("col")
    scal = jnp.concatenate([genetic_var, slab_weight, noise_var])
    everyone = lax.all_gather(dosages, "row", axis=2, tiled=True)
    zr = dosages.reshape(MS, 1024)
    zp = everyone[:, 0, :BOTH]
    zc = lax.dynamic_slice_in_dim(everyone.reshape(MS, 16, 1024), mycol * NB, NB, 2).reshape(MS, 2048)
    block = grm[:, :, 0, :].reshape(1024, NB)
    left = lax.all_gather(block, "col", axis=0)
    p_raw = lax.all_gather(left[:, :NB, :], "row", axis=0)[:8]
    swapped = lax.ppermute(block, ("row", "col"), TRANSPOSE)
    right = lax.all_gather(swapped, "row", axis=0).reshape(16, 8, NB, NB)
    v = factor(scal, p_raw, zp)
    out = update(scal, zr, zp, zc, grm.reshape(1024, 16, NB), left, right, v)
    return out.reshape(grm.shape)


def solution(mesh):
    in_specs = (P(None, "row", None, "col"), P(None, None, "row"), P(), P(), P())
    out_specs = P(None, "row", None, "col")
    return jax.shard_map(
        per_device, mesh=mesh, in_specs=in_specs, out_specs=out_specs, check_vma=False
    )
```

time: 758 us -> 294 us (0.39)
  other arithmetic: 254 us -> 0.08 us
  waiting for transfers between devices: 320 us -> 150 us
  Pallas kernels: 0 us -> 97.7 us
  matrix products: 87.5 us -> 0 us
  local copies, waits for them, and re-layouts: 67.3 us -> 23.5 us
    another operation x37 -> x0, other arithmetic: 239 us -> none  [the longest x29 158 us: per_device(): factor = jnp.linalg.cholesky(diag_block)]
    psum x2 -> x0, waiting for transfers between devices: 233 us -> none  [from_root(): return lax.psum(kept, axis)]
    pallas_call x0 -> x2, Pallas kernels: none -> 97.7 us  [the longest x1 56.5 us: factor(): pl.pallas_call(factor_kernel, out_shape=jax.ShapeDtypeStruct((BOTH, BOTH)...]
    all_gather x2 -> x3, waiting for transfers between devices: 57 us -> 107 us  [the longest x1 65 us: per_device(): p_raw = lax.all_gather(left[:, :NB, :], 'row', axis=0)[:8]]
    another operation x40 -> x0, matrix products: 49.2 us -> none  [the longest x14 35.6 us: per_device(): lax.linalg.triangular_solve(factor, across, left_side=True, lower=True)]
    dot_general x3 -> x0, matrix products: 38.3 us -> none  [the longest x2 33.7 us: per_device(): jnp.dot(left_tail, right_tail, precision=lax.Precision.HIGHEST, preferred...]
    ppermute x0 -> x1, waiting for transfers between devices: none -> 22.8 us  [per_device(): swapped = lax.ppermute(block, ('row', 'col'), TRANSPOSE)]
    reshape x3 -> x1, local copies, waits for them, and re-layouts: 22.7 us -> 2.29 us  [per_device(): everyone.reshape(MS, 16, 1024)]
  transfers between devices with their start and end apart: 5 -> 5, of which waited for: 5 -> 5; matrix products, arithmetic and copies ran while one was open for 4% -> 6% of each run, Pallas kernels for 0% -> 19%
where the time goes in v1:
time: 294 us; the launch traced here: 291 us
  waiting for transfers between devices  150 us (51%)
  Pallas kernels  97.7 us (33%)
  local copies, waits for them, and re-layouts  23.5 us (8%)
  between operations  15.3 us (5%)
  starting transfers between devices  4.01 us (1%)
    all_gather x1, waiting for transfers between devices, per_device(): p_raw = lax.all_gather(left[:, :NB, :], 'row', axis=0)[:8]  65 us
    pallas_call x1, Pallas kernels, factor(): pl.pallas_call(factor_kernel, out_shape=jax.ShapeDtypeStruct((BOTH, BOTH)...  56.5 us
    pallas_call x1, Pallas kernels, update(): pl.pallas_call(update_kernel, out_shape=jax.ShapeDtypeStruct((1024, 16, N...  41.2 us
    all_gather x1, waiting for transfers between devices, per_device(): left = lax.all_gather(block, 'col', axis=0)  32.9 us
    ppermute x1, waiting for transfers between devices, per_device(): swapped = lax.ppermute(block, ('row', 'col'), TRANSPOSE)  22.8 us
    all_gather x1, waiting for transfers between devices, per_device(): everyone = lax.all_gather(dosages, 'row', axis=2, tiled=True)  19.9 us
    all_gather x1, waiting for transfers between devices, per_device(): right = lax.all_gather(swapped, 'row', axis=0).reshape(16, 8, NB, NB)  9.29 us
    unnamed x11, local copies, waits for them, and re-layouts  6.69 us
  transfers between devices with their start and end apart: 5, of which 5 were waited for; matrix products, arithmetic and copies ran while one was open for 6% of the time, Pallas kernels for 19%

profile of v1, /device:TPU:6, one launch (start us, length us, event | category | flops | bytes accessed | tf_op | source)
XLA Modules:
  0.0 290.6 jit_solution(13843731459889375157)
XLA Ops:
  6.5 0.0 all-gather.9.cloned.1.call-start
  6.5 3.3 %slice.13 = f32[8,128,1,128]{3,2,1,0:T(1,128)} slice(f32[8,128,16,128]{3,2,1,0:T(8,128)} %param.5), slice={[0:8], [0:128], [0:1], [0:128]} | slice | bytes 1048576 | tf_op jit(solution)/shard_map/slice | solution.py:280
  9.8 0.0 all-gather.9.cloned.1.call-update
  9.8 0.0 all-gather.7.cloned.1.call-start
  9.9 1.6 copy.9
  11.5 0.0 all-gather.7.cloned.1.call-update
  11.5 0.0 all-gather.13.cloned.1.call-start
  11.6 32.9 %all-gather.9.cloned.1.call-done.left_hbm = f32[8,1024,128]{2,1,0:T(8,128)} async-done(((f32[1,1024,128]{2,1,0:T(8,128)}), f32[8,1024,128]{2,1,0:T(8,128)}) %all-gather.9.cloned.1.call-update) | async-done | bytes 4194320 | tf_op jit(solution)/shard_map/all_gather | solution.py:281
  44.4 1.9 slice.18
  46.3 0.0 all-gather.13.cloned.1.call-update
  46.3 0.0 all-gather.11.cloned.1.call-start
  46.4 3.9 %collective-permute-start = (f32[1024,128]{1,0:T(8,128)}, f32[1024,128]{1,0:T(8,128)S(1)}, u32[]{:S(2)}, u32[]{:S(2)}) collective-permute-start(f32[1024,128]{1,0:T(8,128)} %bitcast.18), channel_id=1, source_target_pairs={{0,0},{1,8},{2,16},{3,24},{4,32},{5,40},{6,48},{7,56},{8,1},{9,9},... | collective-permute-start | bytes 1572872 | tf_op jit(solution)/shard_map/ppermute | solution.py:283
  50.3 22.8 %collective-permute-done = f32[1024,128]{1,0:T(8,128)S(1)} collective-permute-done((f32[1024,128]{1,0:T(8,128)}, f32[1024,128]{1,0:T(8,128)S(1)}, u32[]{:S(2)}, u32[]{:S(2)}) %collective-permute-start) | collective-permute-done | bytes 524320 | tf_op jit(solution)/shard_map/ppermute | solution.py:283
  73.1 0.0 copy-start.3
  73.1 0.8 copy-done.3
  73.9 0.0 all-gather.11.cloned.1.call-update
  75.9 1.6 copy.16
  77.5 0.1 pad_maximum_fusion.scal_ref
  77.5 0.0 copy-start.1
  77.5 19.9 %all-gather.7.cloned.1.call-done = bf16[64,8,2048]{2,0,1:T(8,128)(2,1)} async-done(((bf16[64,8,128]{2,0,1:T(8,128)(2,1)}), bf16[64,8,2048]{2,0,1:T(8,128)(2,1)}) %all-gather.7.cloned.1.call-update) | async-done | bytes 2097168 | tf_op jit(solution)/shard_map/all_gather | solution.py:276
  97.4 2.7 copy.10
  100.2 2.3 reshape.19
  102.4 1.0 constant_dynamic-slice_fusion
  103.4 0.8 copy.15
  104.2 0.9 slice_bitcast_fusion.zp_ref
  105.1 0.0 copy-start
  105.1 65.0 %all-gather.13.cloned.1.call-done = f32[128,128,128]{2,1,0:T(8,128)} async-done(((f32[8,128,128]{2,1,0:T(8,128)}), f32[128,128,128]{2,1,0:T(8,128)}) %all-gather.13.cloned.1.call-update) | async-done | bytes 8388624 | tf_op jit(solution)/shard_map/all_gather | solution.py:282
  170.1 4.7 %slice.19 = f32[64,128,128]{2,1,0:T(8,128)} slice(f32[128,128,128]{2,1,0:T(8,128)} %all-gather.13.cloned.1.call-done), slice={[0:64], [0:128], [0:128]} | slice | bytes 8388608 | tf_op jit(solution)/shard_map/slice | solution.py:282
  174.8 0.0 copy-done.1
  174.8 0.0 copy-done
  174.8 56.5 %panel_factor.1.v_hbm = f32[1024,1024]{1,0:T(8,128)S(1)} custom-call(f32[3]{0:T(128)S(1)} %pad_maximum_fusion.scal_ref, f32[8,8,128,128]{3,2,1,0:T(8,128)} %bitcast.16, bf16[64,1024]{1,0:T(8,128)(2,1)S(1)} %slice_bitcast_fusion.zp_ref), custom_call_target="tpu_custom_call" | custom-call | flops 20000000000 | bytes 8000000 | tf_op jit(solution)/shard_map/panel_factor/pallas_call | solution.py:101
  231.4 0.0 copy-start.2
  231.4 2.0 copy-done.2
  233.3 9.3 %all-gather.11.cloned.1.call-done = f32[16384,128]{1,0:T(8,128)} async-done(((f32[1024,128]{1,0:T(8,128)}), f32[16384,128]{1,0:T(8,128)}) %all-gather.11.cloned.1.call-update) | async-done | bytes 8388624 | tf_op jit(solution)/shard_map/all_gather | solution.py:284
  242.6 41.2 %trailing_update.1 = f32[1024,16,128]{2,1,0:T(8,128)} custom-call(f32[3]{0:T(128)} %copy-done.1, bf16[64,1024]{1,0:T(8,128)(2,1)} %bitcast.22, bf16[64,1024]{1,0:T(8,128)(2,1)} %copy-done, bf16[64,2048]{1,0:T(8,128)(2,1)} %bitcast.21, f32[1024,16,128]{2,1,0:T(8,128)} %bitcast.23, f32[8,1024,128]{2,1,0:T(8,128)} %all-gather.9.cloned.1.call-done.left_hbm, ...), custom_call_target="tpu_custom_call" | custom-call | flops 24999999488 | bytes 36000000 | tf_op jit(solution)/shard_map/trailing_update/pallas_call | solution.py:246
Async XLA Ops:
  6.5 37.9 %all-gather.9.cloned.1.call-start = ((), (), s32[]{:S(2)}) async-start(), calls=%async_computation.1 | async-start | bytes 4718592 | tf_op jit(solution)/shard_map/all_gather | solution.py:281
  9.8 87.6 %all-gather.7.cloned.1.call-start = ((), (), s32[]{:S(2)}) async-start(), calls=%async_computation | async-start | bytes 2228224 | tf_op jit(solution)/shard_map/all_gather | solution.py:276
  11.5 158.6 %all-gather.13.cloned.1.call-start = ((), (), s32[]{:S(2)}) async-start(), calls=%async_computation.3 | async-start | bytes 8912896 | tf_op jit(solution)/shard_map/all_gather | solution.py:282
  46.3 196.3 %all-gather.11.cloned.1.call-start = ((), (), s32[]{:S(2)}) async-start(), calls=%async_computation.2 | async-start | bytes 8912896 | tf_op jit(solution)/shard_map/all_gather | solution.py:284
  46.4 26.7 %collective-permute-start = (f32[1024,128]{1,0:T(8,128)}, f32[1024,128]{1,0:T(8,128)S(1)}, u32[]{:S(2)}, u32[]{:S(2)}) collective-permute-start(f32[1024,128]{1,0:T(8,128)} %bitcast.18), channel_id=1, source_target_pairs={{0,0},{1,8},{2,16},{3,24},{4,32},{5,40},{6,48},{7,56},{8,1},{9,9},... | collective-permute-start | bytes 1572872 | tf_op jit(solution)/shard_map/ppermute | solution.py:283
  73.1 0.8 copy-start.3
  77.5 97.3 %copy-start.1 = (f32[3]{0:T(128)}, f32[3]{0:T(128)S(1)}, u32[]{:S(2)}) copy-start(f32[3]{0:T(128)S(1)} %pad_maximum_fusion.scal_ref) | copy-start | bytes 40
  105.1 69.7 %copy-start = (bf16[64,1024]{1,0:T(8,128)(2,1)}, bf16[64,1024]{1,0:T(8,128)(2,1)S(1)}, u32[]{:S(2)}) copy-start(bf16[64,1024]{1,0:T(8,128)(2,1)S(1)} %slice_bitcast_fusion.zp_ref) | copy-start | bytes 393220
  231.4 2.0 copy-start.2
Sparse Core Ops, SparseCore 0:
  10.0 34.4 all-gather.8
  46.6 50.8 all-gather.6
  99.6 70.5 all-gather.12
  172.1 70.4 all-gather.10

commit v2 on v1

v2 whole, which is shorter than its diff:
```python
import functools

import jax
import jax.numpy as jnp
from jax import lax
from jax.experimental import pallas as pl
from jax.experimental.pallas import tpu as pltpu
from jax.sharding import PartitionSpec as P

NB = 128
MS = 64
PANEL = 512
BOTH = 1024
HI = lax.Precision.HIGHEST
F32 = jnp.float32
BF16 = jnp.bfloat16


def lane_bcast(x, j):
    return jnp.broadcast_to(x[:, j : j + 1], (8, 128))


def sub_bcast(x, i):
    return jnp.broadcast_to(x[i : i + 1, :], (8, 128))


def inverse_factor_128(slabs):
    lane = lax.broadcasted_iota(jnp.int32, (8, 128), 1)
    sub = lax.broadcasted_iota(jnp.int32, (8, 128), 0)
    slabs = list(slabs)
    for s in range(16):
        cols = {t: [lane_bcast(slabs[t], 8 * s + k) for k in range(8)] for t in range(s, 16)}
        b = {(i, k): sub_bcast(cols[s][k], i) for k in range(8) for i in range(k, 8)}
        here = (lane >= 8 * s) & (lane < 8 * s + 8)
        ident = (lane - 8 * s == sub).astype(F32)
        rp = jnp.where(here, ident, slabs[s])
        r = [sub_bcast(rp, i) for i in range(8)]
        inv = [None] * 8
        l = {}
        for j in range(8):
            inv[j] = 1.0 / b[j, j]
            for i in range(j + 1, 8):
                l[i, j] = b[i, j] * inv[j]
            for i in range(j + 1, 8):
                for m in range(j + 1, i + 1):
                    b[i, m] = b[i, m] - l[i, j] * b[m, j]
                r[i] = r[i] - l[i, j] * r[j]
        out = None
        for i in range(8):
            v = r[i] * lax.rsqrt(b[i, i])
            out = v if out is None else jnp.where(sub == i, v, out)
        w = [r[i] * inv[i] for i in range(8)]
        for j in range(7, 0, -1):
            for i in range(j):
                w[i] = w[i] - l[j, i] * w[j]
        slabs[s] = jnp.where(lane < 8 * s + 8, out, 0.0)
        for t in range(s + 1, 16):
            acc = cols[t][0] * w[0]
            for k in range(1, 8):
                acc = acc + cols[t][k] * w[k]
            slabs[t] = jnp.where(here, 0.0, slabs[t]) - acc
    return slabs


NN = (((1,), (0,)), ((), ()))
NT = (((1,), (1,)), ((), ()))
TN = (((0,), (0,)), ((), ()))
MESH = pl.DeviceIdType.MESH
ITEMS = 9


def split(x):
    hi = x.astype(BF16)
    return hi, (x - hi.astype(F32)).astype(BF16)


def dot3(ah, al, bh, bl, dims):
    d = functools.partial(lax.dot_general, dimension_numbers=dims, preferred_element_type=F32)
    return d(ah, bh) + (d(ah, bl) + d(al, bh))


def panel_kernel(
    scal_ref, zr_ref, g_hbm,
    wh, wl, lout, zp_out, left_hbm, right_hbm, zc_hbm,
    v_ref, ps, tmp, blk, zpb, dbuf, vkb, abuf, ah, al, vh, vl,
    xz_send, xz_recv, zp_send, zp_recv, zc_send, zc_recv, c_send, c_recv, q_send, q_recv, loc,
):
    gv, sw, nv = scal_ref[0], scal_ref[1], scal_ref[2]
    swn = sw / MS
    r = lax.axis_index("row")
    c = lax.axis_index("col")
    x, z = r // 4, r % 4
    core = c % 2

    barrier = pltpu.get_barrier_semaphore()
    for o in range(1, 16):
        pl.semaphore_signal(barrier, inc=1, device_id=((r + o) % 16, c), device_id_type=MESH)
    for o in range(1, 8):
        pl.semaphore_signal(barrier, inc=1, device_id=(r, (c + o) % 8), device_id_type=MESH)

    first = pltpu.make_async_copy(g_hbm.at[0:128, 0:8], tmp.at[0:128], loc.at[0])
    rest = pltpu.make_async_copy(g_hbm.at[128:1024, 0:8], tmp.at[128:1024], loc.at[1])
    first.start()
    rest.start()
    slab_copy = pltpu.make_async_copy(g_hbm.at[0:128], right_hbm.at[r % 8], loc.at[2])

    @pl.when(r < 8)
    def _():
        slab_copy.start()

    tmp2 = tmp.reshape(8192, NB)
    first.wait()
    blk[0:NB, :] = tmp2[pl.ds(0, NB, stride=8), :]

    @pl.when(r < 8)
    def _():
        ps[r % 8, c] = blk[0:NB, :]
        zpb[r % 8] = zr_ref[:, 0:NB]

    pl.semaphore_wait(barrier, 22)

    def rdma(src, dst, ssem, rsem, to):
        return pltpu.make_async_remote_copy(
            src_ref=src, dst_ref=dst, send_sem=ssem, recv_sem=rsem, device_id=to, device_id_type=MESH
        )

    rs = r % 8
    xz, zps, zcs = [], [], []
    for n, o in enumerate((8, 4, 12, 2, 6, 10, 14, 1, 3, 5, 7, 9, 11, 13, 15)):
        to = ((r + o) % 16, c)
        xz.append(rdma(ps.at[rs, c], ps.at[rs, c], xz_send.at[n], xz_recv.at[rs], to))
        zps.append(rdma(zpb.at[rs], zpb.at[rs], zp_send.at[n], zp_recv.at[rs], to))
        zcs.append(rdma(zr_ref, zc_hbm.at[r // 8], zc_send.at[n], zc_recv.at[r // 8], to))

    @pl.when(r < 8)
    def _():
        for n in range(15):
            xz[n].start()
        for n in range(15):
            zps[n].start()

    rest.wait()
    for rb in range(1, 8):
        blk[rb * NB : (rb + 1) * NB, :] = tmp2[pl.ds(rb * 1024, NB, stride=8), :]
    left_own = pltpu.make_async_copy(blk, left_hbm.at[c], loc.at[3])
    left_own.start()

    cp, cm, co, sib = (c + 2) % 8, (c + 6) % 8, (c + 4) % 8, c + 1 - 2 * core
    fwd_src = jnp.where(core == 0, cm, cp)
    fwd_to = jnp.where(core == 0, cp, cm)

    def at(i, k):
        return ps.at[i, k] if i < 8 else left_hbm.at[k]

    def gather(i):
        me = lambda k: at(i, k)
        own = blk if i == 8 else me(c)
        return dict(
            plus=rdma(own, me(c), c_send.at[i, 0], c_recv.at[i, 0], (r, cp)),
            minus=rdma(own, me(c), c_send.at[i, 1], c_recv.at[i, 1], (r, cm)),
            fwd=rdma(me(fwd_src), me(fwd_src), c_send.at[i, 2], c_recv.at[i, 2], (r, fwd_to)),
            s0=rdma(own, me(c), c_send.at[i, 3], c_recv.at[i, 3], (r, sib)),
            s1=rdma(me(cm), me(cm), c_send.at[i, 4], c_recv.at[i, 4], (r, sib)),
            s2=rdma(me(cp), me(cp), c_send.at[i, 5], c_recv.at[i, 5], (r, sib)),
            s3=rdma(me(co), me(co), c_send.at[i, 6], c_recv.at[i, 6], (r, sib)),
        )

    items = [gather(i) for i in range(ITEMS)]

    def e0(i):
        if i < 8:
            @pl.when(r != i)
            def _():
                rdma(ps.at[i, c], ps.at[i, c], xz_send.at[0], xz_recv.at[i], (r, sib)).wait_recv()
        for name in ("plus", "minus", "s0"):
            items[i][name].start()

    def e1(i):
        items[i]["plus"].wait_recv()
        items[i]["minus"].wait_recv()
        for name in ("fwd", "s1", "s2"):
            items[i][name].start()

    def e2(i):
        items[i]["fwd"].wait_recv()
        items[i]["s3"].start()

    def e3(i):
        for name in ("s0", "s1", "s2", "s3"):
            items[i][name].wait_recv()

    fs = jnp.where((x == 0) | (x == 3), 0, 1)
    up, down = x * 4 + (z + 1) % 4, x * 4 + (z + 3) % 4
    far = (3 - x) * 4 + z
    partner = (x + 1 - 2 * (x % 2)) * 4 + z

    def part(which, dz, h):
        s = 4 * (fs if which == 0 else 1 - fs) + (z + dz) % 4
        return right_hbm.at[s, :, 8 * h : 8 * h + 8]

    def q(n, h, ref, to):
        return rdma(ref, ref, q_send.at[n, h], q_recv.at[n, h], (to, c))

    Q = []
    for h in range(2):
        f_src = jnp.where(core == 0, (z + 3) % 4, (z + 1) % 4)
        f_to = jnp.where(core == 0, up, down)
        Q.append(
            dict(
                far=q(0, h, part(0, 0, h), far),
                mate=q(1, h, part(0, 0, h), partner),
                fu=q(2, h, part(0, 0, h), up),
                fd=q(3, h, part(0, 0, h), down),
                su=q(4, h, part(1, 0, h), up),
                sd=q(5, h, part(1, 0, h), down),
                ff=q(6, h, right_hbm.at[4 * fs + f_src, :, 8 * h : 8 * h + 8], f_to),
                sf=q(7, h, right_hbm.at[4 * (1 - fs) + f_src, :, 8 * h : 8 * h + 8], f_to),
            )
        )

    def r0():
        @pl.when(x < 2)
        def _():
            slab_copy.wait()
            for h in range(2):
                Q[h]["far"].start()

    def r1(h):
        @pl.when(x >= 2)
        def _():
            Q[h]["far"].wait_recv()
        for name in ("mate", "fu", "fd"):
            Q[h][name].start()

    def r2(h):
        Q[h]["mate"].wait_recv()
        Q[h]["su"].start()
        Q[h]["sd"].start()

    def r3(h):
        Q[h]["fu"].wait_recv()
        Q[h]["fd"].wait_recv()
        Q[h]["ff"].start()

    def r4(h):
        Q[h]["su"].wait_recv()
        Q[h]["sd"].wait_recv()
        Q[h]["sf"].start()

    def r5(h):
        Q[h]["ff"].wait_recv()
        Q[h]["sf"].wait_recv()

    for i in range(8):
        e0(i)
    r0()
    zc_own = pltpu.make_async_copy(zr_ref, zc_hbm.at[r // 8], loc.at[4])

    @pl.when(r % 8 == c)
    def _():
        zc_own.start()
        for n in range(15):
            zcs[n].start()

    for i in range(8):
        @pl.when(r != i)
        def _():
            rdma(zpb.at[i], zpb.at[i], zp_send.at[0], zp_recv.at[i], (r, sib)).wait_recv()
    zp = jnp.concatenate([zpb[i] for i in range(8)], axis=1)
    for i in range(8):
        zp_out[:, i * NB : (i + 1) * NB] = zpb[i]

    service = [
        (lambda: r1(0), ),
        (lambda: r1(1), lambda: e0(8)),
        (lambda: r2(0), ),
        (lambda: r2(1), ),
        (lambda: r3(0), ),
        (lambda: r3(1), ),
        (lambda: r4(0), ),
        (lambda: r4(1), ),
    ]

    def prepare(k):
        kb = k * NB
        n = BOTH - kb
        s = lax.dot_general(zp[:, kb : kb + NB], zp[:, kb:], TN, preferred_element_type=F32)
        g = jnp.concatenate([ps[k, j] for j in range(k, 8)], axis=1)
        on = lax.broadcasted_iota(jnp.int32, (NB, n), 0) == lax.broadcasted_iota(jnp.int32, (NB, n), 1)
        a = gv * (g + swn * s) + jnp.where(on, nv, 0.0)
        if k > 0:
            a = a + v_ref[kb : kb + NB, kb:]
        v_ref[kb : kb + NB, kb:] = a
        dbuf[...] = a[:, :NB]

    e1(0)
    e1(1)
    e2(0)
    e3(0)
    prepare(0)

    @pl.loop(0, 8)
    def _(k):
        slabs = [dbuf[8 * s : 8 * s + 8, :] for s in range(16)]
        for s, v in enumerate(inverse_factor_128(slabs)):
            vkb[8 * s : 8 * s + 8, :] = v
        for kk in range(8):
            @pl.when(k == kk)
            def _():
                kb = kk * NB
                vk = vkb[...]
                parts = []
                if kk > 0:
                    parts.append(jnp.dot(vk, v_ref[kb : kb + NB, :kb], precision=HI, preferred_element_type=F32))
                parts.append(vk)
                if kk < 7:
                    right = jnp.dot(vk, v_ref[kb : kb + NB, kb + NB :], precision=HI, preferred_element_type=F32)
                    parts.append(right)
                    u = jnp.concatenate(parts, axis=1)
                    upd = lax.dot_general(right, u, TN, precision=HI, preferred_element_type=F32)
                    if kk > 0:
                        v_ref[kb + NB :, :kb] = v_ref[kb + NB :, :kb] - upd[:, :kb]
                        v_ref[kb : kb + NB, :kb] = parts[0]
                        v_ref[kb + NB :, kb + NB :] = v_ref[kb + NB :, kb + NB :] - upd[:, kb + NB :]
                    else:
                        v_ref[kb + NB :, kb + NB :] = -upd[:, kb + NB :]
                    v_ref[kb + NB :, kb : kb + NB] = -upd[:, kb : kb + NB]
                    v_ref[kb : kb + NB, kb : kb + NB] = vk
                    v_ref[kb : kb + NB, kb + NB :] = jnp.zeros((NB, BOTH - kb - NB), F32)
                else:
                    v_ref[kb : kb + NB, :] = jnp.concatenate(parts, axis=1)
                for f in service[kk]:
                    f()
                if kk + 2 < ITEMS:
                    e1(kk + 2)
                if kk + 1 < ITEMS:
                    e2(kk + 1)
                if kk + 1 < 8:
                    e3(kk + 1)
                    prepare(kk + 1)

    left_own.wait()
    e3(8)
    pulls = [
        pltpu.make_async_copy(left_hbm.at[k], abuf.at[:, k * NB : (k + 1) * NB], loc.at[5 + k]) for k in range(8)
    ]
    for p in pulls:
        p.start()
    for J in range(4):
        js = slice(J * 256, (J + 1) * 256)
        h, lo = split(v_ref[js, :])
        vh[js, :] = h
        vl[js, :] = lo
    for p in pulls:
        p.wait()

    @pl.loop(0, 8)
    def _(rb):
        rows = pl.ds(pl.multiple_of(rb * NB, NB), NB)
        s = lax.dot_general(zr_ref[:, rows], zp_out[...], TN, preferred_element_type=F32)
        r_at = lax.broadcasted_iota(jnp.int32, (NB, BOTH), 0) + (r + 16 * rb) * NB
        c_at = lax.broadcasted_iota(jnp.int32, (NB, BOTH), 1)
        a = gv * (abuf[rows, :] + swn * s) + jnp.where(r_at == c_at, nv, 0.0)
        h, lo = split(a)
        ah[rows, :] = h
        al[rows, :] = lo

    for J in range(4):
        K = (J + 1) * 256
        js = slice(J * 256, (J + 1) * 256)
        abuf[:, js] = dot3(ah[:, :K], al[:, :K], vh[js, :K], vl[js, :K], NT)

    keep1 = jnp.where(r >= 4, 1.0, 0.0)
    keep2 = jnp.where(r >= 8, 1.0, 0.0)
    for rb in range(8):
        rows = slice(rb * NB, (rb + 1) * NB)
        a = abuf[rows, :]
        if rb == 0:
            c_at = lax.broadcasted_iota(jnp.int32, (NB, BOTH), 1)
            a = a * jnp.where(c_at < PANEL, keep1, keep2)
        h, lo = split(a)
        ah[rows, :] = h
        al[rows, :] = lo
    lout[...] = abuf[:, pl.ds(pl.multiple_of(c * NB, NB), NB)]

    for J in range(4):
        js = slice(J * 256, (J + 1) * 256)
        K = slice(J * 256, BOTH)
        h, lo = split(dot3(ah[:, K], al[:, K], vh[K, js], vl[K, js], NN))
        wh[:, js] = h
        wl[:, js] = lo

    for h in range(2):
        r5(h)

    @pl.when(r < 8)
    def _():
        for n in range(15):
            xz[n].wait_send()
            zps[n].wait_send()

    @pl.when(r % 8 == c)
    def _():
        zc_own.wait()
        for n in range(15):
            zcs[n].wait_send()

    for hh in range(2):
        @pl.when(r != c + 8 * hh)
        def _():
            rdma(zr_ref, zc_hbm.at[hh], zc_send.at[0], zc_recv.at[hh], (r, sib)).wait_recv()
    for i in range(ITEMS):
        for name in items[i]:
            items[i][name].wait_send()
    for h in range(2):
        @pl.when(x < 2)
        def _():
            Q[h]["far"].wait_send()
        for name in ("mate", "fu", "fd", "su", "sd", "ff", "sf"):
            Q[h][name].wait_send()


def panels(scal, zr, g):
    hbm = pl.BlockSpec(memory_space=pl.ANY)
    vmem = pl.BlockSpec(memory_space=pltpu.VMEM)
    dma = pltpu.SemaphoreType.DMA
    return pl.pallas_call(
        panel_kernel,
        out_shape=[
            jax.ShapeDtypeStruct((1024, BOTH), BF16),
            jax.ShapeDtypeStruct((1024, BOTH), BF16),
            jax.ShapeDtypeStruct((1024, NB), F32),
            jax.ShapeDtypeStruct((MS, BOTH), BF16),
            jax.ShapeDtypeStruct((8, 1024, NB), F32),
            jax.ShapeDtypeStruct((8, NB, 16, NB), F32),
            jax.ShapeDtypeStruct((2, MS, 1024), BF16),
        ],
        in_specs=[pl.BlockSpec(memory_space=pltpu.SMEM), vmem, hbm],
        out_specs=[vmem, vmem, vmem, vmem, hbm, hbm, hbm],
        scratch_shapes=[
            pltpu.VMEM((BOTH, BOTH), F32),
            pltpu.VMEM((8, 8, NB, NB), F32),
            pltpu.VMEM((1024, 8, NB), F32),
            pltpu.VMEM((1024, NB), F32),
            pltpu.VMEM((8, MS, NB), BF16),
            pltpu.VMEM((NB, NB), F32),
            pltpu.VMEM((NB, NB), F32),
            pltpu.VMEM((1024, BOTH), F32),
            pltpu.VMEM((1024, BOTH), BF16),
            pltpu.VMEM((1024, BOTH), BF16),
            pltpu.VMEM((BOTH, BOTH), BF16),
            pltpu.VMEM((BOTH, BOTH), BF16),
            dma((15,)), dma((8,)), dma((15,)), dma((8,)), dma((15,)), dma((2,)),
            dma((ITEMS, 7)), dma((ITEMS, 7)), dma((8, 2)), dma((8, 2)), dma((13,)),
        ],
        compiler_params=pltpu.CompilerParams(
            vmem_limit_bytes=60 * 1024 * 1024, collective_id=0, has_side_effects=True
        ),
        cost_estimate=pl.CostEstimate(flops=30_000_000_000, bytes_accessed=30_000_000, transcendentals=0),
        name="panel_factor",
    )(scal, zr, g)


def update_kernel(
    scal_ref, zr_ref, zp_ref, zc_ref, lblk_ref, g_hbm, right_hbm, wh_hbm, wl_hbm, out_hbm,
    gbuf, rbuf, wh, wl, sems,
):
    gv, sw, nv = scal_ref[0], scal_ref[1], scal_ref[2]
    swn = sw / MS
    row = lax.axis_index("row")
    col = lax.axis_index("col")
    loads = [
        pltpu.make_async_copy(wh_hbm, wh, sems.at[0]),
        pltpu.make_async_copy(wl_hbm, wl, sems.at[1]),
        pltpu.make_async_copy(right_hbm, rbuf, sems.at[2]),
        pltpu.make_async_copy(g_hbm, gbuf, sems.at[3]),
    ]
    for d in loads:
        d.start()
    for d in loads:
        d.wait()
    zr = zr_ref[...]
    zp = zp_ref[...]
    g2 = gbuf.reshape(16384, NB)
    r2 = rbuf.reshape(16384, NB)

    @pl.loop(0, 8)
    def _(p):
        where = pl.ds(pl.multiple_of(p * NB, NB), NB)
        zc = jnp.concatenate([zc_ref[0, :, where], zc_ref[1, :, where]], axis=1)
        s = lax.dot_general(zp, zc, TN, preferred_element_type=F32)
        raw = jnp.concatenate([r2[pl.ds(2 * p + e, BOTH, stride=16), :] for e in range(2)], axis=1)
        rh, rl = split(gv * (raw + swn * s))
        upd = dot3(wh[...], wl[...], rh, rl, NN)
        own = lax.dot_general(zr, zc, TN, preferred_element_type=F32)
        eye = jnp.where(
            lax.broadcasted_iota(jnp.int32, (NB, NB), 0) == lax.broadcasted_iota(jnp.int32, (NB, NB), 1), nv, 0.0
        )
        for rb in range(8):
            rows = slice(rb * NB, (rb + 1) * NB)
            for e in range(2):
                es = slice(e * NB, (e + 1) * NB)
                lc = 2 * p + e
                at = pl.ds(rb * 2048 + lc, NB, stride=16)
                on = jnp.where(16 * rb + row == 8 * lc + col, 1.0, 0.0)
                g2[at, :] = gv * (g2[at, :] + swn * own[rows, es]) - upd[rows, es] + on * eye

    r_at = lax.broadcasted_iota(jnp.int32, (NB, NB), 0) + row * NB
    c_at = lax.broadcasted_iota(jnp.int32, (NB, NB), 1) + col * NB
    for rb in range(8):
        x = lblk_ref[rb * NB : (rb + 1) * NB, :]
        if rb == 0:
            x = jnp.where(r_at >= c_at, x, 0.0)
        g2[pl.ds(rb * 2048, NB, stride=16), :] = x
    done = pltpu.make_async_copy(gbuf, out_hbm, sems.at[4])
    done.start()
    done.wait()


def update(scal, zr, zp, zc, lblk, g, right, wh, wl):
    hbm = pl.BlockSpec(memory_space=pl.ANY)
    vmem = pl.BlockSpec(memory_space=pltpu.VMEM)
    return pl.pallas_call(
        update_kernel,
        out_shape=jax.ShapeDtypeStruct((1024, 16, NB), F32),
        in_specs=[pl.BlockSpec(memory_space=pltpu.SMEM), vmem, vmem, vmem, vmem, hbm, hbm, hbm, hbm],
        out_specs=hbm,
        scratch_shapes=[
            pltpu.VMEM((1024, 16, NB), F32),
            pltpu.VMEM((1024, 16, NB), F32),
            pltpu.VMEM((1024, BOTH), BF16),
            pltpu.VMEM((1024, BOTH), BF16),
            pltpu.SemaphoreType.DMA((5,)),
        ],
        compiler_params=pltpu.CompilerParams(vmem_limit_bytes=60 * 1024 * 1024),
        cost_estimate=pl.CostEstimate(flops=15_000_000_000, bytes_accessed=30_000_000, transcendentals=0),
        name="trailing_update",
    )(scal, zr, zp, zc, lblk, g, right, wh, wl)


def per_device(grm, dosages, slab_weight, genetic_var, noise_var):
    scal = jnp.concatenate([genetic_var, slab_weight, noise_var])
    zr = dosages.reshape(MS, 1024)
    g = grm.reshape(1024, 16, NB)
    wh, wl, lblk, zp, _, right, zc = panels(scal, zr, g)
    out = update(scal, zr, zp, zc, lblk, g, right.reshape(1024, 16, NB), wh, wl)
    return out.reshape(grm.shape)


def solution(mesh):
    in_specs = (P(None, "row", None, "col"), P(None, None, "row"), P(), P(), P())
    out_specs = P(None, "row", None, "col")
    return jax.shard_map(
        per_device, mesh=mesh, in_specs=in_specs, out_specs=out_specs, check_vma=False
    )
```

time: 294 us -> 179 us (0.61)
  waiting for transfers between devices: 150 us -> 0 us
  Pallas kernels: 97.7 us -> 172 us
  local copies, waits for them, and re-layouts: 23.5 us -> 1.59 us
  between operations: 15.3 us -> 2.11 us
  starting transfers between devices: 4.01 us -> 0 us
    all_gather x4 -> x0, waiting for transfers between devices: 127 us -> none  [the longest x1 65 us: per_device(): p_raw = lax.all_gather(left[:, :NB, :], 'row', axis=0)[:8]]
    pallas_call x1, Pallas kernels: 56.5 us -> 137 us  [panels(): pl.pallas_call(panel_kernel, out_shape=[jax.ShapeDtypeStruct((1024, BOTH)...]
    ppermute x1 -> x0, waiting for transfers between devices: 22.8 us -> none  [per_device(): swapped = lax.ppermute(block, ('row', 'col'), TRANSPOSE)]
    slice x3 -> x0, local copies, waits for them, and re-layouts: 9.86 us -> none  [the longest x2 6.57 us: per_device(): p_raw = lax.all_gather(left[:, :NB, :], 'row', axis=0)[:8]]
    pallas_call x1, Pallas kernels: 41.2 us -> 34.5 us  [update(): pl.pallas_call(update_kernel, out_shape=jax.ShapeDtypeStruct((1024, 16, N...]
    unnamed x11 -> x1, local copies, waits for them, and re-layouts: 6.69 us -> 1.59 us
    ppermute x1 -> x0, starting transfers between devices: 3.88 us -> none  [per_device(): swapped = lax.ppermute(block, ('row', 'col'), TRANSPOSE)]
  transfers between devices with their start and end apart: 5 -> 0, of which waited for: 5 -> 0; matrix products, arithmetic and copies ran while one was open for 6% -> 0% of each run, Pallas kernels for 19% -> 0%
where the time goes in v2:
time: 179 us; the launch traced here: 176 us
  Pallas kernels  172 us (96%)
  between operations  2.11 us (1%)
    pallas_call x1, Pallas kernels, panels(): pl.pallas_call(panel_kernel, out_shape=[jax.ShapeDtypeStruct((1024, BOTH)...  137 us
    pallas_call x1, Pallas kernels, update(): pl.pallas_call(update_kernel, out_shape=jax.ShapeDtypeStruct((1024, 16, N...  34.5 us

profile of v2, /device:TPU:6, one launch (start us, length us, event | category | flops | bytes accessed | tf_op | source)
XLA Modules:
  0.0 176.2 jit_solution(6458341419628121770)
XLA Ops:
  1.9 0.7 pad_maximum_fusion.scal_ref
  2.6 1.6 copy.8
  4.2 137.3 %panel_factor.1 = (bf16[1024,1024]{1,0:T(8,128)(2,1)}, bf16[1024,1024]{1,0:T(8,128)(2,1)}, f32[1024,128]{1,0:T(8,128)}, bf16[64,1024]{1,0:T(8,128)(2,1)}, f32[8,...) custom-call(f32[3]{0:T(128)} %pad_maximum_fusion.scal_ref, bf16[64,1024]{1,0:T(8,128)(2,1)} %bitcast.8, ...), custom_call_target="tpu_custom_call" | custom-call | flops 30000001024 | bytes 30000000 | tf_op jit(solution)/shard_map/panel_factor/pallas_call | solution.py:427
  141.5 34.5 %trailing_update.1 = f32[1024,16,128]{2,1,0:T(8,128)} custom-call(f32[3]{0:T(128)} %pad_maximum_fusion.scal_ref, bf16[64,1024]{1,0:T(8,128)(2,1)} %bitcast.9, bf16[64,1024]{1,0:T(8,128)(2,1)} %get-tuple-element.11.zp_ref, bf16[2,64,1024]{2,1,0:T(8,128)(2,1)} %get-tuple-element.12.zc_ref, f32[1024,128]{1,0:T(8,128)} %get-tuple-element.13.lblk_ref, ...), custom_call_target="tpu_custom_call" | custom-call | flops 15000000512 | bytes 30000000 | tf_op jit(solution)/shard_map/trailing_update/pallas_call | solution.py:523

commit v3 on v2

v3 whole, which is shorter than its diff:
```python
import functools

import jax
import jax.numpy as jnp
from jax import lax
from jax.experimental import pallas as pl
from jax.experimental.pallas import tpu as pltpu
from jax.sharding import PartitionSpec as P

NB = 128
MS = 64
PANEL = 512
BOTH = 1024
F32 = jnp.float32
BF16 = jnp.bfloat16


def lane_bcast(x, j):
    return jnp.broadcast_to(x[:, j : j + 1], (8, 128))


def sub_bcast(x, i):
    return jnp.broadcast_to(x[i : i + 1, :], (8, 128))


def inverse_factor_128(slabs):
    lane = lax.broadcasted_iota(jnp.int32, (8, 128), 1)
    sub = lax.broadcasted_iota(jnp.int32, (8, 128), 0)
    slabs = list(slabs)
    for s in range(16):
        cols = {t: [lane_bcast(slabs[t], 8 * s + k) for k in range(8)] for t in range(s, 16)}
        b = {(i, k): sub_bcast(cols[s][k], i) for k in range(8) for i in range(k, 8)}
        here = (lane >= 8 * s) & (lane < 8 * s + 8)
        ident = (lane - 8 * s == sub).astype(F32)
        rp = jnp.where(here, ident, slabs[s])
        r = [sub_bcast(rp, i) for i in range(8)]
        inv = [None] * 8
        l = {}
        if s < 15:
            nx = jnp.where(here, 0.0, slabs[s + 1])
            cn = list(cols[s + 1])
        for j in range(0, 8, 2):
            a, e, f = b[j, j], b[j + 1, j], b[j + 1, j + 1]
            rd = 1.0 / (a * f - e * e)
            inv[j] = 1.0 / a
            l[j + 1, j] = e * inv[j]
            inv[j + 1] = a * rd
            m0, m1 = {}, {}
            for i in range(j + 2, 8):
                m0[i] = (b[i, j] * f - b[i, j + 1] * e) * rd
                m1[i] = (b[i, j + 1] * a - b[i, j] * e) * rd
                l[i, j] = b[i, j] * inv[j]
                l[i, j + 1] = m1[i]
            for i in range(j + 2, 8):
                for m in range(j + 2, i + 1):
                    b[i, m] = b[i, m] - (m0[i] * b[m, j] + m1[i] * b[m, j + 1])
            for i in range(j + 2, 8):
                r[i] = r[i] - (m0[i] * r[j] + m1[i] * r[j + 1])
            if s < 15:
                q0 = (cn[j] * f - cn[j + 1] * e) * rd
                q1 = (cn[j + 1] * a - cn[j] * e) * rd
                nx = nx - (q0 * r[j] + q1 * r[j + 1])
                for i in range(j + 2, 8):
                    cn[i] = cn[i] - (m0[i] * cn[j] + m1[i] * cn[j + 1])
            r[j + 1] = r[j + 1] - l[j + 1, j] * r[j]
            b[j + 1, j + 1] = f - l[j + 1, j] * e
        out = None
        for i in range(8):
            v = r[i] * lax.rsqrt(b[i, i])
            out = v if out is None else jnp.where(sub == i, v, out)
        w = [r[i] * inv[i] for i in range(8)]
        for j in range(7, 0, -1):
            for i in range(j):
                w[i] = w[i] - l[j, i] * w[j]
        slabs[s] = jnp.where(lane < 8 * s + 8, out, 0.0)
        if s < 15:
            slabs[s + 1] = nx
        for t in range(s + 2, 16):
            acc = cols[t][0] * w[0]
            for k in range(1, 8):
                acc = acc + cols[t][k] * w[k]
            slabs[t] = jnp.where(here, 0.0, slabs[t]) - acc
    return slabs


NN = (((1,), (0,)), ((), ()))
NT = (((1,), (1,)), ((), ()))
TN = (((0,), (0,)), ((), ()))
MESH = pl.DeviceIdType.MESH
ITEMS = 9


def split(x):
    hi = x.astype(BF16)
    return hi, (x - hi.astype(F32)).astype(BF16)


def dot3(ah, al, bh, bl, dims):
    d = functools.partial(lax.dot_general, dimension_numbers=dims, preferred_element_type=F32)
    return d(ah, bh) + (d(ah, bl) + d(al, bh))


def panel_kernel(
    gv_ref, sw_ref, nv_ref, zr_ref, g_hbm,
    out_hbm,
    v_ref, ps, gbuf, blk, zpb, zcb, dbuf, vkb, lbuf, rbuf, abuf, ah, al, vh, vl, wh, wl, rh, rl, ub,
    xz_send, xz_recv, zp_send, zp_recv, zc_send, zc_recv, c_send, c_recv, q_send, q_recv, loc,
):
    gv, sw, nv = gv_ref[0], sw_ref[0], nv_ref[0]
    swn = sw / MS
    r = lax.axis_index("row")
    c = lax.axis_index("col")
    x, z = r // 4, r % 4
    core = c % 2

    barrier = pltpu.get_barrier_semaphore()
    for o in range(1, 16):
        pl.semaphore_signal(barrier, inc=1, device_id=((r + o) % 16, c), device_id_type=MESH)
    for o in range(1, 8):
        pl.semaphore_signal(barrier, inc=1, device_id=(r, (c + o) % 8), device_id_type=MESH)

    first = pltpu.make_async_copy(g_hbm.at[0:128], gbuf.at[0:128], loc.at[0])
    rest = pltpu.make_async_copy(g_hbm.at[128:1024], gbuf.at[128:1024], loc.at[1])
    first.start()
    rest.start()
    slab_copy = pltpu.make_async_copy(g_hbm.at[0:128], rbuf.at[r % 8], loc.at[2])

    @pl.when(r < 8)
    def _():
        slab_copy.start()

    g2 = gbuf.reshape(16384, NB)
    first.wait()
    blk[0:NB, :] = g2[pl.ds(0, NB, stride=16), :]

    @pl.when(r < 8)
    def _():
        ps[r % 8, c] = blk[0:NB, :]
        zpb[r % 8] = zr_ref[:, 0:NB]

    pl.semaphore_wait(barrier, 22)

    def rdma(src, dst, ssem, rsem, to):
        return pltpu.make_async_remote_copy(
            src_ref=src, dst_ref=dst, send_sem=ssem, recv_sem=rsem, device_id=to, device_id_type=MESH
        )

    rs = r % 8
    xz, zps, zcs = [], [], []
    for n, o in enumerate((8, 4, 12, 2, 6, 10, 14, 1, 3, 5, 7, 9, 11, 13, 15)):
        to = ((r + o) % 16, c)
        xz.append(rdma(ps.at[rs, c], ps.at[rs, c], xz_send.at[n], xz_recv.at[rs], to))
        zps.append(rdma(zpb.at[rs], zpb.at[rs], zp_send.at[n], zp_recv.at[rs], to))
        zcs.append(rdma(zr_ref, zcb.at[r // 8], zc_send.at[n], zc_recv.at[r // 8], to))

    @pl.when(r == 0)
    def _():
        for n in range(15):
            xz[n].start()

    @pl.when(r < 8)
    def _():
        for n in range(15):
            zps[n].start()

    def own_rows():
        rest.wait()
        for rb in range(1, 8):
            blk[rb * NB : (rb + 1) * NB, :] = g2[pl.ds(rb * 2048, NB, stride=16), :]
        lbuf[c] = blk[...]

    cp, cm, co, sib = (c + 2) % 8, (c + 6) % 8, (c + 4) % 8, c + 1 - 2 * core
    fwd_src = jnp.where(core == 0, cm, cp)
    fwd_to = jnp.where(core == 0, cp, cm)

    def at(i, k):
        return ps.at[i, k] if i < 8 else lbuf.at[k]

    def gather(i):
        me = lambda k: at(i, k)
        own = blk if i == 8 else me(c)
        return dict(
            plus=rdma(own, me(c), c_send.at[i, 0], c_recv.at[i, 0], (r, cp)),
            minus=rdma(own, me(c), c_send.at[i, 1], c_recv.at[i, 1], (r, cm)),
            fwd=rdma(me(fwd_src), me(fwd_src), c_send.at[i, 2], c_recv.at[i, 2], (r, fwd_to)),
            s0=rdma(own, me(c), c_send.at[i, 3], c_recv.at[i, 3], (r, sib)),
            s1=rdma(me(cm), me(cm), c_send.at[i, 4], c_recv.at[i, 4], (r, sib)),
            s2=rdma(me(cp), me(cp), c_send.at[i, 5], c_recv.at[i, 5], (r, sib)),
            s3=rdma(me(co), me(co), c_send.at[i, 6], c_recv.at[i, 6], (r, sib)),
        )

    items = [gather(i) for i in range(ITEMS)]

    def e0(i):
        if i < 8:
            @pl.when(r != i)
            def _():
                rdma(ps.at[i, c], ps.at[i, c], xz_send.at[0], xz_recv.at[i], (r, sib)).wait_recv()
        for name in ("plus", "minus", "s0"):
            items[i][name].start()

    def e1(i):
        items[i]["plus"].wait_recv()
        items[i]["minus"].wait_recv()
        for name in ("fwd", "s1", "s2"):
            items[i][name].start()

    def e2(i):
        items[i]["fwd"].wait_recv()
        items[i]["s3"].start()

    def e3(i):
        for name in ("s0", "s1", "s2", "s3"):
            items[i][name].wait_recv()

    fs = jnp.where((x == 0) | (x == 3), 0, 1)
    up, down = x * 4 + (z + 1) % 4, x * 4 + (z + 3) % 4
    far = (3 - x) * 4 + z
    partner = (x + 1 - 2 * (x % 2)) * 4 + z

    def part(which, dz, h):
        s = 4 * (fs if which == 0 else 1 - fs) + (z + dz) % 4
        return rbuf.at[s, :, 8 * h : 8 * h + 8]

    def q(n, h, ref, to):
        return rdma(ref, ref, q_send.at[n, h], q_recv.at[n, h], (to, c))

    Q = []
    for h in range(2):
        f_src = jnp.where(core == 0, (z + 3) % 4, (z + 1) % 4)
        f_to = jnp.where(core == 0, up, down)
        Q.append(
            dict(
                far=q(0, h, part(0, 0, h), far),
                mate=q(1, h, part(0, 0, h), partner),
                fu=q(2, h, part(0, 0, h), up),
                fd=q(3, h, part(0, 0, h), down),
                su=q(4, h, part(1, 0, h), up),
                sd=q(5, h, part(1, 0, h), down),
                ff=q(6, h, rbuf.at[4 * fs + f_src, :, 8 * h : 8 * h + 8], f_to),
                sf=q(7, h, rbuf.at[4 * (1 - fs) + f_src, :, 8 * h : 8 * h + 8], f_to),
            )
        )

    def r0():
        @pl.when(x < 2)
        def _():
            slab_copy.wait()
            for h in range(2):
                Q[h]["far"].start()

    def r1(h):
        @pl.when(x >= 2)
        def _():
            Q[h]["far"].wait_recv()
        for name in ("mate", "fu", "fd"):
            Q[h][name].start()

    def r2(h):
        Q[h]["mate"].wait_recv()
        Q[h]["su"].start()
        Q[h]["sd"].start()

    def r3(h):
        Q[h]["fu"].wait_recv()
        Q[h]["fd"].wait_recv()
        Q[h]["ff"].start()

    def r4(h):
        Q[h]["su"].wait_recv()
        Q[h]["sd"].wait_recv()
        Q[h]["sf"].start()

    def r5(h):
        Q[h]["ff"].wait_recv()
        Q[h]["sf"].wait_recv()

    e0(0)

    @pl.when((r > 0) & (r < 8))
    def _():
        for n in range(15):
            xz[n].start()

    zc_own = pltpu.make_async_copy(zr_ref, zcb.at[r // 8], loc.at[4])

    def share_dosages():
        @pl.when(r % 8 == c)
        def _():
            zc_own.start()
            for n in range(15):
                zcs[n].start()

    for i in range(8):
        @pl.when(r != i)
        def _():
            rdma(zpb.at[i], zpb.at[i], zp_send.at[0], zp_recv.at[i], (r, sib)).wait_recv()
    zp = jnp.concatenate([zpb[i] for i in range(8)], axis=1)

    early = [
        (lambda: e2(1), lambda: e1(2), lambda: e0(3)),
        (lambda: e0(5), lambda: e2(3), own_rows, lambda: e0(8)),
        (lambda: e0(7), lambda: e2(4)),
        (lambda: e2(5),),
        (lambda: e2(6), lambda: e1(8)),
        (lambda: e2(7),),
        (lambda: e2(8),),
        (),
    ]
    late = [
        (lambda: e0(4), lambda: e2(2), lambda: e1(3), share_dosages, lambda: r1(0)),
        (lambda: e0(6), lambda: e1(4), lambda: r1(1)),
        (lambda: e1(5), lambda: r2(0)),
        (lambda: e1(6), lambda: r2(1)),
        (lambda: e1(7), lambda: r3(0)),
        (lambda: r3(1),),
        (lambda: r4(0),),
        (lambda: r4(1),),
    ]

    def prepare(k):
        kb = k * NB
        n = BOTH - kb
        s = lax.dot_general(zp[:, kb : kb + NB], zp[:, kb:], TN, preferred_element_type=F32)
        g = jnp.concatenate([ps[k, j] for j in range(k, 8)], axis=1)
        on = lax.broadcasted_iota(jnp.int32, (NB, n), 0) == lax.broadcasted_iota(jnp.int32, (NB, n), 1)
        a = gv * (g + swn * s) + jnp.where(on, nv, 0.0)
        if k > 0:
            a = a + v_ref[kb : kb + NB, kb:]
        v_ref[kb : kb + NB, kb:] = a
        dbuf[...] = a[:, :NB]

    e1(0)
    e0(1)
    e2(0)
    e0(2)
    e1(1)
    e3(0)
    prepare(0)
    r0()

    @pl.loop(0, 8)
    def _(k):
        slabs = [dbuf[8 * s : 8 * s + 8, :] for s in range(16)]
        for s, v in enumerate(inverse_factor_128(slabs)):
            vkb[8 * s : 8 * s + 8, :] = v
        for kk in range(8):
            @pl.when(k == kk)
            def _():
                kb = kk * NB
                for f in early[kk]:
                    f()
                vk = vkb[...]
                parts = []
                if kk > 0:
                    parts.append(dot3(*split(vk), *split(v_ref[kb : kb + NB, :kb]), NN))
                parts.append(vk)
                if kk < 7:
                    right = dot3(*split(vk), *split(v_ref[kb : kb + NB, kb + NB :]), NN)
                    parts.append(right)
                    u = jnp.concatenate(parts, axis=1)
                    upd = dot3(*split(right), *split(u), TN)
                    if kk > 0:
                        v_ref[kb + NB :, :kb] = v_ref[kb + NB :, :kb] - upd[:, :kb]
                        v_ref[kb : kb + NB, :kb] = parts[0]
                        v_ref[kb + NB :, kb + NB :] = v_ref[kb + NB :, kb + NB :] - upd[:, kb + NB :]
                    else:
                        v_ref[kb + NB :, kb + NB :] = -upd[:, kb + NB :]
                    v_ref[kb + NB :, kb : kb + NB] = -upd[:, kb : kb + NB]
                    v_ref[kb : kb + NB, kb : kb + NB] = vk
                    v_ref[kb : kb + NB, kb + NB :] = jnp.zeros((NB, BOTH - kb - NB), F32)
                else:
                    v_ref[kb : kb + NB, :] = jnp.concatenate(parts, axis=1)
                for f in late[kk]:
                    f()
                if kk + 1 < 8:
                    e3(kk + 1)
                    prepare(kk + 1)

    e3(8)
    for J in range(4):
        js = slice(J * 256, (J + 1) * 256)
        h, lo = split(v_ref[js, :])
        vh[js, :] = h
        vl[js, :] = lo

    @pl.loop(0, 8)
    def _(rb):
        rows = pl.ds(pl.multiple_of(rb * NB, NB), NB)
        s = lax.dot_general(zr_ref[:, rows], jnp.concatenate([zpb[i] for i in range(8)], axis=1), TN, preferred_element_type=F32)
        r_at = lax.broadcasted_iota(jnp.int32, (NB, BOTH), 0) + (r + 16 * rb) * NB
        c_at = lax.broadcasted_iota(jnp.int32, (NB, BOTH), 1)
        a = gv * (jnp.concatenate([lbuf[k, rows, :] for k in range(8)], axis=1) + swn * s) + jnp.where(r_at == c_at, nv, 0.0)
        h, lo = split(a)
        ah[rows, :] = h
        al[rows, :] = lo

    for J in range(4):
        K = (J + 1) * 256
        js = slice(J * 256, (J + 1) * 256)
        abuf[:, js] = dot3(ah[:, :K], al[:, :K], vh[js, :K], vl[js, :K], NT)

    keep1 = jnp.where(r >= 4, 1.0, 0.0)
    keep2 = jnp.where(r >= 8, 1.0, 0.0)
    for rb in range(8):
        rows = slice(rb * NB, (rb + 1) * NB)
        a = abuf[rows, :]
        if rb == 0:
            c_at = lax.broadcasted_iota(jnp.int32, (NB, BOTH), 1)
            a = a * jnp.where(c_at < PANEL, keep1, keep2)
        h, lo = split(a)
        ah[rows, :] = h
        al[rows, :] = lo

    for J in range(4):
        js = slice(J * 256, (J + 1) * 256)
        K = slice(J * 256, BOTH)
        h, lo = split(dot3(ah[:, K], al[:, K], vh[K, js], vl[K, js], NN))
        wh[:, js] = h
        wl[:, js] = lo

    for hh in range(2):
        @pl.when(r != c + 8 * hh)
        def _():
            rdma(zr_ref, zcb.at[hh], zc_send.at[0], zc_recv.at[hh], (r, sib)).wait_recv()

    @pl.when(r % 8 == c)
    def _():
        zc_own.wait()

    r2v = rbuf.reshape(16384, NB)
    zr = zr_ref[...]
    eye = jnp.where(
        lax.broadcasted_iota(jnp.int32, (NB, NB), 0) == lax.broadcasted_iota(jnp.int32, (NB, NB), 1), nv, 0.0
    )
    stores = [
        pltpu.make_async_copy(gbuf.at[:, 8 * h : 8 * h + 8], out_hbm.at[:, 8 * h : 8 * h + 8], loc.at[h])
        for h in range(2)
    ]
    for half in range(2):
        r5(half)

        @pl.loop(4 * half, 4 * half + 4)
        def _(p):
            where = pl.ds(pl.multiple_of(p * NB, NB), NB)
            zc = jnp.concatenate([zcb[0, :, where], zcb[1, :, where]], axis=1)
            s = lax.dot_general(zp, zc, TN, preferred_element_type=F32)
            for e in range(2):
                es = slice(e * NB, (e + 1) * NB)
                raw = r2v[pl.ds(2 * p + e, BOTH, stride=16), :]
                hi, lo = split(gv * (raw + swn * s[:, es]))
                rh[:, es] = hi
                rl[:, es] = lo
            ub[...] = dot3(wh[...], wl[...], rh[...], rl[...], NN)
            own = lax.dot_general(zr, zc, TN, preferred_element_type=F32)
            for rb in range(8):
                rows = slice(rb * NB, (rb + 1) * NB)
                for e in range(2):
                    es = slice(e * NB, (e + 1) * NB)
                    lc = 2 * p + e
                    place = pl.ds(rb * 2048 + lc, NB, stride=16)
                    on = jnp.where(16 * rb + r == 8 * lc + c, 1.0, 0.0)
                    g2[place, :] = gv * (g2[place, :] + swn * own[rows, es]) - ub[rows, es] + on * eye

        if half == 0:
            mine = pl.ds(pl.multiple_of(c * NB, NB), NB)
            r_at = lax.broadcasted_iota(jnp.int32, (NB, NB), 0) + r * NB
            c_at = lax.broadcasted_iota(jnp.int32, (NB, NB), 1) + c * NB
            for rb in range(8):
                a = abuf[rb * NB : (rb + 1) * NB, mine]
                if rb == 0:
                    a = jnp.where(r_at >= c_at, a, 0.0)
                g2[pl.ds(rb * 2048, NB, stride=16), :] = a
        stores[half].start()
    for d in stores:
        d.wait()

    @pl.when(r < 8)
    def _():
        for n in range(15):
            xz[n].wait_send()
            zps[n].wait_send()

    @pl.when(r % 8 == c)
    def _():
        for n in range(15):
            zcs[n].wait_send()

    for i in range(ITEMS):
        for name in items[i]:
            items[i][name].wait_send()
    for h in range(2):
        @pl.when(x < 2)
        def _():
            Q[h]["far"].wait_send()
        for name in ("mate", "fu", "fd", "su", "sd", "ff", "sf"):
            Q[h][name].wait_send()


def factored(scal, zr, g):
    hbm = pl.BlockSpec(memory_space=pl.ANY)
    vmem = pl.BlockSpec(memory_space=pltpu.VMEM)
    dma = pltpu.SemaphoreType.DMA
    return pl.pallas_call(
        panel_kernel,
        out_shape=jax.ShapeDtypeStruct((1024, 16, NB), F32),
        in_specs=[pl.BlockSpec(memory_space=pltpu.SMEM)] * 3 + [vmem, hbm],
        out_specs=hbm,
        scratch_shapes=[
            pltpu.VMEM((BOTH, BOTH), F32),
            pltpu.VMEM((8, 8, NB, NB), F32),
            pltpu.VMEM((1024, 16, NB), F32),
            pltpu.VMEM((1024, NB), F32),
            pltpu.VMEM((8, MS, NB), BF16),
            pltpu.VMEM((2, MS, 1024), BF16),
            pltpu.VMEM((NB, NB), F32),
            pltpu.VMEM((NB, NB), F32),
            pltpu.VMEM((8, 1024, NB), F32),
            pltpu.VMEM((8, NB, 16, NB), F32),
            pltpu.VMEM((1024, BOTH), F32),
            pltpu.VMEM((1024, BOTH), BF16),
            pltpu.VMEM((1024, BOTH), BF16),
            pltpu.VMEM((BOTH, BOTH), BF16),
            pltpu.VMEM((BOTH, BOTH), BF16),
            pltpu.VMEM((1024, BOTH), BF16),
            pltpu.VMEM((1024, BOTH), BF16),
            pltpu.VMEM((BOTH, 256), BF16),
            pltpu.VMEM((BOTH, 256), BF16),
            pltpu.VMEM((1024, 256), F32),
            dma((15,)), dma((8,)), dma((15,)), dma((8,)), dma((15,)), dma((2,)),
            dma((ITEMS, 7)), dma((ITEMS, 7)), dma((8, 2)), dma((8, 2)), dma((5,)),
        ],
        compiler_params=pltpu.CompilerParams(
            vmem_limit_bytes=62 * 1024 * 1024, collective_id=0, has_side_effects=True
        ),
        cost_estimate=pl.CostEstimate(flops=45_000_000_000, bytes_accessed=18_000_000, transcendentals=0),
        name="panel_factor",
    )(*scal, zr, g)


def per_device(grm, dosages, slab_weight, genetic_var, noise_var):
    scal = (genetic_var, slab_weight, noise_var)
    return factored(scal, dosages.reshape(MS, 1024), grm.reshape(1024, 16, NB)).reshape(grm.shape)


def solution(mesh):
    in_specs = (P(None, "row", None, "col"), P(None, None, "row"), P(), P(), P())
    out_specs = P(None, "row", None, "col")
    return jax.shard_map(
        per_device, mesh=mesh, in_specs=in_specs, out_specs=out_specs, check_vma=False
    )
```

time: 179 us -> 150 us (0.84)
  Pallas kernels: 172 us -> 137 us
  local copies, waits for them, and re-layouts: 1.59 us -> 8.9 us
    pallas_call x2 -> x1, Pallas kernels: 172 us -> 137 us  [factored(): pl.pallas_call(panel_kernel, out_shape=jax.ShapeDtypeStruct((1024, 16, NB...]
    unnamed x1 -> x2, local copies, waits for them, and re-layouts: 1.59 us -> 8.9 us
where the time goes in v3:
time: 150 us; the launch traced here: 148 us
  Pallas kernels  137 us (91%)
  local copies, waits for them, and re-layouts  8.9 us (6%)
  between operations  1.95 us (1%)
    pallas_call x1, Pallas kernels, factored(): pl.pallas_call(panel_kernel, out_shape=jax.ShapeDtypeStruct((1024, 16, NB...  137 us
    unnamed x2, local copies, waits for them, and re-layouts  8.9 us

profile of v3, /device:TPU:6, one launch (start us, length us, event | category | flops | bytes accessed | tf_op | source)
XLA Modules:
  0.0 147.6 jit_solution(2551286693697311558)
XLA Ops:
  1.9 1.6 %copy.8 = bf16[8,8,8,128]{3,1,2,0:T(8,128)(2,1)} copy(bf16[8,8,8,128]{3,2,1,0:T(8,128)(2,1)} %bitcast.7) | data formatting | bytes 262144
  3.5 136.7 %panel_factor.1 = f32[1024,16,128]{2,1,0:T(8,128)} custom-call(f32[1]{0:T(128)S(6)} %copy.11.gv_ref, f32[1]{0:T(128)S(6)} %copy.10.sw_ref, f32[1]{0:T(128)S(6)} %copy.12.nv_ref, bf16[64,1024]{1,0:T(8,128)(2,1)} %bitcast.8, f32[1024,16,128]{2,1,0:T(8,128)} %bitcast.9), custom_call_target="tpu_custom_call" | custom-call | flops 44999999488 | bytes 18000000 | tf_op jit(solution)/shard_map/panel_factor/pallas_call | solution.py:504
  140.3 7.3 %copy.13 = f32[8,128,16,128]{3,2,1,0:T(8,128)} copy(f32[8,128,16,128]{3,2,1,0:T(8,128)} %bitcast.6) | data formatting | bytes 16777216

commit v4 on v3

--- a/solution.py
+++ b/solution.py
@@ -122,15 +122,16 @@
     first = pltpu.make_async_copy(g_hbm.at[0:128], gbuf.at[0:128], loc.at[0])
     rest = pltpu.make_async_copy(g_hbm.at[128:1024], gbuf.at[128:1024], loc.at[1])
     first.start()
-    rest.start()
     slab_copy = pltpu.make_async_copy(g_hbm.at[0:128], rbuf.at[r % 8], loc.at[2])
-
-    @pl.when(r < 8)
-    def _():
-        slab_copy.start()
 
     g2 = gbuf.reshape(16384, NB)
     first.wait()
+    rest.start()
+
+    @pl.when(r < 8)
+    def _():
+        slab_copy.start()
+
     blk[0:NB, :] = g2[pl.ds(0, NB, stride=16), :]
 
     @pl.when(r < 8)
@@ -153,7 +154,7 @@
         zps.append(rdma(zpb.at[rs], zpb.at[rs], zp_send.at[n], zp_recv.at[rs], to))
         zcs.append(rdma(zr_ref, zcb.at[r // 8], zc_send.at[n], zc_recv.at[r // 8], to))
 
-    @pl.when(r == 0)
+    @pl.when(r < 3)
     def _():
         for n in range(15):
             xz[n].start()
@@ -238,23 +239,31 @@
                 su=q(4, h, part(1, 0, h), up),
                 sd=q(5, h, part(1, 0, h), down),
                 ff=q(6, h, rbuf.at[4 * fs + f_src, :, 8 * h : 8 * h + 8], f_to),
-                sf=q(7, h, rbuf.at[4 * (1 - fs) + f_src, :, 8 * h : 8 * h + 8], f_to),
+                xf=q(7, h, part(0, 2, h), partner),
             )
         )
 
-    def r0():
+    def r0(h):
         @pl.when(x < 2)
         def _():
-            slab_copy.wait()
-            for h in range(2):
-                Q[h]["far"].start()
+            if h == 0:
+                slab_copy.wait()
+            Q[h]["far"].start()
+
+    def r1a(h):
+        @pl.when(x < 2)
+        def _():
+            spread(h)
+
+    def spread(h):
+        for name in ("mate", "fu", "fd"):
+            Q[h][name].start()
 
     def r1(h):
         @pl.when(x >= 2)
         def _():
             Q[h]["far"].wait_recv()
-        for name in ("mate", "fu", "fd"):
-            Q[h][name].start()
+            spread(h)
 
     def r2(h):
         Q[h]["mate"].wait_recv()
@@ -267,21 +276,24 @@
         Q[h]["ff"].start()
 
     def r4(h):
+        Q[h]["ff"].wait_recv()
+        Q[h]["xf"].start()
+
+    def r5(h):
         Q[h]["su"].wait_recv()
         Q[h]["sd"].wait_recv()
-        Q[h]["sf"].start()
-
-    def r5(h):
-        Q[h]["ff"].wait_recv()
-        Q[h]["sf"].wait_recv()
-
+        Q[h]["xf"].wait_recv()
+
+    r0(0)
     e0(0)
 
-    @pl.when((r > 0) & (r < 8))
+    @pl.when((r >= 3) & (r < 8))
     def _():
         for n in range(15):
             xz[n].start()
 
+    r0(1)
+    r1a(0)
     zc_own = pltpu.make_async_copy(zr_ref, zcb.at[r // 8], loc.at[4])
 
     def share_dosages():
@@ -298,24 +310,24 @@
     zp = jnp.concatenate([zpb[i] for i in range(8)], axis=1)
 
     early = [
-        (lambda: e2(1), lambda: e1(2), lambda: e0(3)),
-        (lambda: e0(5), lambda: e2(3), own_rows, lambda: e0(8)),
-        (lambda: e0(7), lambda: e2(4)),
-        (lambda: e2(5),),
-        (lambda: e2(6), lambda: e1(8)),
-        (lambda: e2(7),),
-        (lambda: e2(8),),
+        (lambda: e2(1), lambda: e1(2), lambda: e0(3), lambda: r1(0)),
+        (lambda: e0(5), lambda: e1(3)),
+        (lambda: e0(7), lambda: e1(5)),
+        (lambda: e1(6),),
+        (),
+        (),
+        (),
         (),
     ]
     late = [
-        (lambda: e0(4), lambda: e2(2), lambda: e1(3), share_dosages, lambda: r1(0)),
-        (lambda: e0(6), lambda: e1(4), lambda: r1(1)),
-        (lambda: e1(5), lambda: r2(0)),
-        (lambda: e1(6), lambda: r2(1)),
-        (lambda: e1(7), lambda: r3(0)),
-        (lambda: r3(1),),
-        (lambda: r4(0),),
-        (lambda: r4(1),),
+        (lambda: e0(4), lambda: e2(2), share_dosages, lambda: r1a(1)),
+        (lambda: e0(6), lambda: e1(4), lambda: e2(3), lambda: r1(1)),
+        (lambda: e2(4), lambda: r3(0), lambda: r2(0)),
+        (lambda: e1(7), lambda: e2(5), own_rows, lambda: e0(8)),
+        (lambda: e2(6), lambda: r3(1), lambda: r2(1)),
+        (lambda: e2(7), lambda: e1(8)),
+        (lambda: e2(8), lambda: r4(0)),
+        (),
     ]
 
     def prepare(k):
@@ -337,7 +349,6 @@
     e1(1)
     e3(0)
     prepare(0)
-    r0()
 
     @pl.loop(0, 8)
     def _(k):
@@ -400,6 +411,8 @@
         js = slice(J * 256, (J + 1) * 256)
         abuf[:, js] = dot3(ah[:, :K], al[:, :K], vh[js, :K], vl[js, :K], NT)
 
+    r4(1)
+
     keep1 = jnp.where(r >= 4, 1.0, 0.0)
     keep2 = jnp.where(r >= 8, 1.0, 0.0)
     for rb in range(8):
@@ -493,7 +506,7 @@
         @pl.when(x < 2)
         def _():
             Q[h]["far"].wait_send()
-        for name in ("mate", "fu", "fd", "su", "sd", "ff", "sf"):
+        for name in ("mate", "fu", "fd", "su", "sd", "ff", "xf"):
             Q[h][name].wait_send()
 
 

time: 150 us -> 141 us (0.940); the launches traced: 148 us -> 141 us
  Pallas kernels: 137 us -> 130 us
    pallas_call x1, Pallas kernels: 137 us -> 130 us  [factored(): pl.pallas_call(panel_kernel, out_shape=jax.ShapeDtypeStruct((1024, 16, NB...]
where the time goes in v4:
time: 141 us
  Pallas kernels  130 us (92%)
  local copies, waits for them, and re-layouts  8.9 us (6%)
  between operations  1.95 us (1%)
    pallas_call x1, Pallas kernels, factored(): pl.pallas_call(panel_kernel, out_shape=jax.ShapeDtypeStruct((1024, 16, NB...  130 us
    unnamed x2, local copies, waits for them, and re-layouts  8.9 us

profile of v4, /device:TPU:6, one launch (start us, length us, event | category | flops | bytes accessed | tf_op | source)
XLA Modules:
  0.0 140.5 jit_solution(1634233179974039815)
XLA Ops:
  1.9 1.6 %copy.8 = bf16[8,8,8,128]{3,1,2,0:T(8,128)(2,1)} copy(bf16[8,8,8,128]{3,2,1,0:T(8,128)(2,1)} %bitcast.7) | data formatting | bytes 262144
  3.5 129.7 %panel_factor.1 = f32[1024,16,128]{2,1,0:T(8,128)} custom-call(f32[1]{0:T(128)S(6)} %copy.11.gv_ref, f32[1]{0:T(128)S(6)} %copy.10.sw_ref, f32[1]{0:T(128)S(6)} %copy.12.nv_ref, bf16[64,1024]{1,0:T(8,128)(2,1)} %bitcast.8, f32[1024,16,128]{2,1,0:T(8,128)} %bitcast.9), custom_call_target="tpu_custom_call" | custom-call | flops 44999999488 | bytes 18000000 | tf_op jit(solution)/shard_map/panel_factor/pallas_call | solution.py:517
  133.2 7.3 %copy.13 = f32[8,128,16,128]{3,2,1,0:T(8,128)} copy(f32[8,128,16,128]{3,2,1,0:T(8,128)} %bitcast.6) | data formatting | bytes 16777216

commit v5 on v4

--- a/solution.py
+++ b/solution.py
@@ -388,17 +388,17 @@
                     e3(kk + 1)
                     prepare(kk + 1)
 
-    e3(8)
     for J in range(4):
         js = slice(J * 256, (J + 1) * 256)
         h, lo = split(v_ref[js, :])
         vh[js, :] = h
         vl[js, :] = lo
+    e3(8)
 
     @pl.loop(0, 8)
     def _(rb):
         rows = pl.ds(pl.multiple_of(rb * NB, NB), NB)
-        s = lax.dot_general(zr_ref[:, rows], jnp.concatenate([zpb[i] for i in range(8)], axis=1), TN, preferred_element_type=F32)
+        s = lax.dot_general(zr_ref[:, rows], zp, TN, preferred_element_type=F32)
         r_at = lax.broadcasted_iota(jnp.int32, (NB, BOTH), 0) + (r + 16 * rb) * NB
         c_at = lax.broadcasted_iota(jnp.int32, (NB, BOTH), 1)
         a = gv * (jnp.concatenate([lbuf[k, rows, :] for k in range(8)], axis=1) + swn * s) + jnp.where(r_at == c_at, nv, 0.0)

time: 141 us -> 141 us (level)
  no operation moved by 1% of the time
where the time goes in v5:
time: 141 us
  Pallas kernels  130 us (92%)
  local copies, waits for them, and re-layouts  8.9 us (6%)
  between operations  1.95 us (1%)
    pallas_call x1, Pallas kernels, factored(): pl.pallas_call(panel_kernel, out_shape=jax.ShapeDtypeStruct((1024, 16, NB...  130 us
    unnamed x2, local copies, waits for them, and re-layouts  8.9 us

profile of v5, /device:TPU:6, one launch (start us, length us, event | category | flops | bytes accessed | tf_op | source)
XLA Modules:
  0.0 140.5 jit_solution(12916680473940769271)
XLA Ops:
  1.9 1.6 %copy.8 = bf16[8,8,8,128]{3,1,2,0:T(8,128)(2,1)} copy(bf16[8,8,8,128]{3,2,1,0:T(8,128)(2,1)} %bitcast.7) | data formatting | bytes 262144
  3.5 129.7 %panel_factor.1 = f32[1024,16,128]{2,1,0:T(8,128)} custom-call(f32[1]{0:T(128)S(6)} %copy.11.gv_ref, f32[1]{0:T(128)S(6)} %copy.10.sw_ref, f32[1]{0:T(128)S(6)} %copy.12.nv_ref, bf16[64,1024]{1,0:T(8,128)(2,1)} %bitcast.8, f32[1024,16,128]{2,1,0:T(8,128)} %bitcast.9), custom_call_target="tpu_custom_call" | custom-call | flops 44999999488 | bytes 18000000 | tf_op jit(solution)/shard_map/panel_factor/pallas_call | solution.py:517
  133.2 7.3 %copy.13 = f32[8,128,16,128]{3,2,1,0:T(8,128)} copy(f32[8,128,16,128]{3,2,1,0:T(8,128)} %bitcast.6) | data formatting | bytes 16777216
